TPU v7x, 32 devices: a whole 2x2x4 slice. The times are simulated.
32 devices in a mesh: wall: 16 (over z, x, core), span: 2 (over y).
Axes of the slice: x: 2, y: 2, z: 4, core: 2. Of those that a mesh axis runs over, the one named last changes fastest.
Arguments:
- heat_content: float32 [192, 512, 256], P(None, 'wall', 'span'), may hold values from -6 to 6
- interval_index: int32 [192, 512, 256], P(None, 'wall', 'span'), may hold values from 0 to 15
- wall_matrix: float32 [512, 512], replicated, as said below
- base_temp: float32 [16], replicated, may hold values from -1 to 1
- enth_offset: float32 [16], replicated, may hold values from -0.5 to 0.5
- slope: float32 [16], replicated, may hold values from 0.2 to 1
- curvature: float32 [16], replicated, may hold values from 2 to 20
Outputs:
- heat_content_next: float32 [192, 512, 256], P(None, 'wall', 'span')
- thermal_state: float32 [192, 512, 256], P(None, 'wall', 'span')
Inputs may be any that keep to these rules, and one draw needn't show every extreme that they name: wall_matrix[511 - i, 511 - j] = -wall_matrix[i, j] for all i, j.
All inputs are finite; a program needn't handle non-finite values.
Results may differ from a plain program's by a relative error of at most 0.0003.
Values sent between devices are 32-bit elements; how exact they have to be, the bound alone decides.
No kernel may reach another device: no remote copies, remote signals or barrier semaphores. Data moves between devices by JAX's collectives and lax.ppermute only.
A program may use at most 128 MiB of HBM per device.

v0:
```python
import jax
import jax.numpy as jnp
from jax import lax
from jax.sharding import PartitionSpec as P

NEWTON = 4


time_step = 0.4
gamma_one = 8.0 / 15.0
gamma_two = 5.0 / 12.0
zeta_two = -17.0 / 60.0


def padded(block, sides, width):
    for axis, dim in sides:
        count = lax.axis_size(axis)
        forward = [(i, i + 1) for i in range(count - 1)]
        forward.append((count - 1, 0))
        backward = [(target, source) for source, target in forward]
        low = lax.ppermute(
            lax.slice_in_dim(block, block.shape[dim] - width, None, axis=dim), axis, forward
        )
        high = lax.ppermute(lax.slice_in_dim(block, 0, width, axis=dim), axis, backward)
        block = jnp.concatenate([low, block, high], axis=dim)
    return block


def lookup(table, interval_index):
    indices = lax.broadcasted_iota(jnp.int32, (table.shape[0],) + interval_index.shape, 0)
    shaped = table.reshape((-1,) + (1,) * interval_index.ndim)
    return jnp.sum(
        jnp.where(interval_index[None] == indices, shaped, jnp.zeros_like(shaped)), axis=0
    )


def invert_heat_content(
    grid_entries, interval_lower_edge, interval_shift, first_power_factor, third_power_factor
):
    remainder = grid_entries - interval_shift
    offset_temp = remainder / first_power_factor
    for sweep in range(NEWTON):
        cubic_part = third_power_factor * offset_temp * offset_temp
        mismatch = first_power_factor * offset_temp + cubic_part * offset_temp - remainder
        slope_now = first_power_factor + 3.0 * cubic_part
        offset_temp = offset_temp - mismatch / slope_now
    return interval_lower_edge + offset_temp


def heat_conductance(thermal_estimate):
    return 0.5 + 1.0 / (1.0 + thermal_estimate * thermal_estimate)


def crosswise_contribution(extended_array):
    conduct_pad = heat_conductance(extended_array)
    upper = (
        0.5
        * (conduct_pad[..., 1:-1] + conduct_pad[..., 2:])
        * (extended_array[..., 2:] - extended_array[..., 1:-1])
    )
    lower = (
        0.5
        * (conduct_pad[..., :-2] + conduct_pad[..., 1:-1])
        * (extended_array[..., 1:-1] - extended_array[..., :-2])
    )
    return upper - lower


def on_device(heat_content, interval_index, wall_matrix, base_temp, enth_offset, slope, curvature):
    interval_lower_edge = lookup(base_temp, interval_index)
    interval_shift = lookup(enth_offset, interval_index)
    first_power_factor = lookup(slope, interval_index)
    third_power_factor = lookup(curvature, interval_index)

    def boundary_operator(pencil):
        return jnp.einsum(
            "ij,pjz->piz",
            wall_matrix,
            pencil,
            precision=lax.Precision.HIGHEST,
            preferred_element_type=jnp.float32,
        )

    def rate(grid_entries):
        thermal_estimate = invert_heat_content(
            grid_entries,
            interval_lower_edge,
            interval_shift,
            first_power_factor,
            third_power_factor,
        )
        pencil = lax.all_to_all(thermal_estimate, "wall", split_axis=0, concat_axis=1, tiled=True)
        inner = heat_conductance(pencil) * boundary_operator(pencil)
        boundary_contribution = lax.all_to_all(
            boundary_operator(inner), "wall", split_axis=1, concat_axis=0, tiled=True
        )
        extended_array = padded(thermal_estimate, (("span", 2),), 1)
        return (boundary_contribution + crosswise_contribution(extended_array), thermal_estimate)

    first_rate, first_temp = rate(heat_content)
    section = heat_content + time_step * gamma_one * first_rate
    second_rate, second_temp = rate(section)
    final = section + time_step * (gamma_two * second_rate + zeta_two * first_rate)
    return (final, second_temp)


def solution(mesh):
    in_specs = (P(None, "wall", "span"), P(None, "wall", "span"), P(), P(), P(), P(), P())
    out_specs = (P(None, "wall", "span"), P(None, "wall", "span"))
    return jax.shard_map(
        on_device, mesh=mesh, in_specs=in_specs, out_specs=out_specs, check_vma=False
    )
```

profile of v0, /device:TPU:11, one launch (start us, length us, event | category | flops | bytes accessed | tf_op | source)
XLA Modules:
  0.0 482.8 jit_solution(192353345686541103)
XLA Ops:
  0.6 26.3 %select_reduce_fusion.2 = (f32[192,32,128]{2,1,0:T(8,128)S(1)}, f32[192,32,128]{2,1,0:T(8,128)}, f32[192,32,128]{2,1,0:T(8,128)}, f32[192,32,128]{2,1,0:T(8,128)}) fusion(f32[16]{0:T(128)} %param.11, s32[192,32,128]{2,1,0:T(8,128)} %param.8, f32[16]{0:T(128)} %param.13, f32[16]{0:T(128)} %param.12, f32[16]{0:T(128)} %param.10), kind=kLoop, calls=%fused_computation.2 | loop fusion | flops 110100480 | bytes 15728896 | tf_op jit(solution)/shard_map/reduce_sum | solution.py:32
  26.9 8.6 %fusion.39 = f32[192,32,128]{2,1,0:T(8,128)S(1)} fusion(f32[192,32,128]{2,1,0:T(8,128)} %get-tuple-element.5, f32[192,32,128]{2,1,0:T(8,128)} %get-tuple-element.4, f32[192,32,128]{2,1,0:T(8,128)} %get-tuple-element.3, f32[192,32,128]{2,1,0:T(8,128)} %param.7, f32[192,32,128]{2,1,0:T(8,128)S(1)} %get-tuple-element.2), kind=kLoop, calls=%fused_computation.69 | loop fusion | flops 30670848 | bytes 18874368 | tf_op jit(solution)/shard_map/add | solution.py:47
  35.5 76.1 %all_to_all.72 = f32[192,32,128]{2,1,0:T(8,128)S(1)} all-to-all(f32[192,32,128]{2,1,0:T(8,128)S(1)} %fusion.39), channel_id=1, replica_groups=mesh['wall'=16,'span'=2] {'wall'}, dimensions={0} | all-to-all | bytes 6291456 | tf_op jit(solution)/shard_map/all_to_all | solution.py:92
  113.6 4.0 copy.56
  117.6 12.3 %fusion.64 = f32[12,128,512]{2,1,0:T(8,128)S(1)} fusion(f32[12,512,128]{2,1,0:T(8,128)} %bitcast.45, f32[512,512]{1,0:T(8,128)S(1)} %copy-done), kind=kOutput, calls=%fused_computation.98 | convolution fusion | flops 4831838208 | bytes 7340032 | tf_op jit(solution)/shard_map/ij,pjz->piz/dot_general | solution.py:76
  130.0 7.4 %fusion.54 = f32[12,512,128]{1,2,0:T(8,128)} fusion(f32[12,128,512]{2,1,0:T(8,128)S(1)} %fusion.64, f32[12,512,128]{1,2,0:T(8,128)S(1)} %copy-done.9, f32[512,512]{1,0:T(8,128)S(1)} %copy-done), kind=kOutput, calls=%fused_computation.88 | convolution fusion | flops 4835770368 | bytes 10485760 | tf_op jit(solution)/shard_map/ij,pjz->piz/dot_general | solution.py:76
  137.4 5.1 %copy.59 = f32[12,512,128]{2,0,1:T(8,128)} copy(f32[12,512,128]{1,2,0:T(8,128)} %fusion.54) | data formatting | bytes 6291456 | tf_op jit(solution)/shard_map/ij,pjz->piz/transpose | solution.py:76
  142.5 5.2 %all-to-all-start.1 = ((f32[12,512,128]{2,0,1:T(8,128)}), f32[12,512,128]{2,0,1:T(8,128)}, u32[]{:S(2)}, u32[]{:S(2)}) async-start(f32[12,512,128]{2,0,1:T(8,128)} %copy.59), calls=%async_computation.1 | async-start | bytes 8388608 | tf_op jit(solution)/shard_map/all_to_all | solution.py:94
  147.7 6.4 %fusion.72 = (f32[192,32,1]{2,1,0:T(8,128)}, f32[192,32,1]{2,1,0:T(8,128)}) fusion(f32[192,32,128]{2,1,0:T(8,128)} %copy-done.1), kind=kLoop, calls=%fused_computation.105 | loop fusion | bytes 98304 | tf_op jit(solution)/shard_map/slice | solution.py:24
  167.1 7.0 %fusion.2 = f32[192,32,130]{2,1,0:T(8,128)} fusion(f32[192,32,1]{2,1,0:T(8,128)} %copy.65, f32[192,32,128]{2,1,0:T(8,128)} %copy-done.1, f32[192,32,1]{2,1,0:T(8,128)} %copy.64), kind=kLoop, calls=%fused_computation.8 | loop fusion | flops 4792320 | bytes 6389760 | tf_op jit(solution)/shard_map/add | solution.py:51
  174.1 66.0 %all-to-all-done.1 = f32[12,512,128]{2,0,1:T(8,128)} async-done(((f32[12,512,128]{2,0,1:T(8,128)}), f32[12,512,128]{2,0,1:T(8,128)}, u32[]{:S(2)}, u32[]{:S(2)}) %all-to-all-start.1) | async-done | bytes 3145760 | tf_op jit(solution)/shard_map/all_to_all | solution.py:94
  240.2 3.3 copy.61
  244.3 17.8 %fusion.30 = (f32[192,32,128]{2,1,0:T(8,128)S(1)}, f32[192,32,128]{2,1,0:T(8,128)}) fusion(f32[192,32,128]{2,1,0:T(8,128)} %get-tuple-element.5, f32[192,32,128]{2,1,0:T(8,128)} %get-tuple-element.4, f32[192,32,128]{2,1,0:T(8,128)} %get-tuple-element.3, f32[192,32,128]{2,1,0:T(8,128)S(1)} %copy-done.7, f32[192,32,128]{2,1,0:T(8,128)} %param.7, ...), kind=kLoop, calls=%fused_computation.56 | loop fusion | flops 41680896 | bytes 37797888 | tf_op jit(solution)/shard_map/add | solution.py:47
  262.1 74.7 %all_to_all.73 = f32[192,32,128]{2,1,0:T(8,128)S(1)} all-to-all(f32[192,32,128]{2,1,0:T(8,128)S(1)} %get-tuple-element.6), channel_id=1, replica_groups=mesh['wall'=16,'span'=2] {'wall'}, dimensions={0} | all-to-all | bytes 6291456 | tf_op jit(solution)/shard_map/all_to_all | solution.py:92
  338.9 12.1 %fusion.61 = f32[12,128,512]{2,1,0:T(8,128)} fusion(f32[12,512,128]{2,1,0:T(8,128)S(1)} %bitcast.46, f32[512,512]{1,0:T(8,128)S(1)} %copy-done), kind=kOutput, calls=%fused_computation.95 | convolution fusion | flops 4831838208 | bytes 7340032 | tf_op jit(solution)/shard_map/ij,pjz->piz/dot_general | solution.py:76
  351.1 3.6 copy.69
  354.6 9.1 %fusion.55 = f32[12,512,128]{1,2,0:T(8,128)} fusion(f32[12,128,512]{2,1,0:T(8,128)} %fusion.61, f32[12,512,128]{1,2,0:T(8,128)} %copy.69, f32[512,512]{1,0:T(8,128)S(1)} %copy-done), kind=kOutput, calls=%fused_computation.89 | convolution fusion | flops 4835770368 | bytes 10485760 | tf_op jit(solution)/shard_map/ij,pjz->piz/dot_general | solution.py:76
  363.8 5.1 %copy.72 = f32[12,512,128]{2,0,1:T(8,128)} copy(f32[12,512,128]{1,2,0:T(8,128)} %fusion.55) | data formatting | bytes 6291456 | tf_op jit(solution)/shard_map/ij,pjz->piz/transpose | solution.py:76
  368.8 5.2 %all-to-all-start.3 = ((f32[12,512,128]{2,0,1:T(8,128)}), f32[12,512,128]{2,0,1:T(8,128)}, u32[]{:S(2)}, u32[]{:S(2)}) async-start(f32[12,512,128]{2,0,1:T(8,128)} %copy.72), calls=%async_computation.3 | async-start | bytes 8388608 | tf_op jit(solution)/shard_map/all_to_all | solution.py:94
  374.0 6.4 %fusion.71 = (f32[192,32,1]{2,1,0:T(8,128)}, f32[192,32,1]{2,1,0:T(8,128)}) fusion(f32[192,32,128]{2,1,0:T(8,128)} %copy-done.3), kind=kLoop, calls=%fused_computation.104 | loop fusion | bytes 98304 | tf_op jit(solution)/shard_map/slice | solution.py:24
  393.3 7.0 %fusion.5 = f32[192,32,130]{2,1,0:T(8,128)} fusion(f32[192,32,1]{2,1,0:T(8,128)} %copy.78, f32[192,32,128]{2,1,0:T(8,128)} %copy-done.3, f32[192,32,1]{2,1,0:T(8,128)} %copy.77), kind=kLoop, calls=%fused_computation.12 | loop fusion | flops 4792320 | bytes 6389760 | tf_op jit(solution)/shard_map/add | solution.py:51
  400.4 66.1 %all-to-all-done.3 = f32[12,512,128]{2,0,1:T(8,128)} async-done(((f32[12,512,128]{2,0,1:T(8,128)}), f32[12,512,128]{2,0,1:T(8,128)}, u32[]{:S(2)}, u32[]{:S(2)}) %all-to-all-start.3) | async-done | bytes 3145760 | tf_op jit(solution)/shard_map/all_to_all | solution.py:94
  466.5 3.3 copy.74
  470.6 11.8 %fusion.13 = f32[192,32,128]{2,1,0:T(8,128)} fusion(f32[192,32,128]{2,1,0:T(8,128)S(1)} %copy-done.4, f32[192,32,1]{2,1,0:T(8,128)} %copy.77, f32[192,32,130]{2,1,0:T(8,128)} %fusion.5, f32[192,32,1]{2,1,0:T(8,128)S(1)} %copy-done.8, f32[16,12,32,128]{3,2,1,0:T(8,128)S(1)} %copy.74, f32[192,32,128]{2,1,0:T(8,128)} %get-tuple-element.7, f32[192,32,128]{2,1,0:T(8,128)} %param.7), kind=kLoop, calls=%fused_computation.29 | loop fusion | flops 14942208 | bytes 25214976 | tf_op jit(solution)/shard_map/add | solution.py:103
  (38 shorter events, 31.6 us)
Async XLA Ops:
  0.6 117.0 %copy-start = (f32[512,512]{1,0:T(8,128)S(1)}, f32[512,512]{1,0:T(8,128)}, u32[]{:S(2)}) copy-start(f32[512,512]{1,0:T(8,128)} %param.9) | copy-start | bytes 3145732
  26.9 8.6 %copy-start.6 = (f32[192,32,128]{2,1,0:T(8,128)}, f32[192,32,128]{2,1,0:T(8,128)S(1)}, u32[]{:S(2)}) copy-start(f32[192,32,128]{2,1,0:T(8,128)S(1)} %get-tuple-element.2) | copy-start | bytes 9437188
  35.5 76.1 %copy-start.1 = (f32[192,32,128]{2,1,0:T(8,128)}, f32[192,32,128]{2,1,0:T(8,128)S(1)}, u32[]{:S(2)}) copy-start(f32[192,32,128]{2,1,0:T(8,128)S(1)} %fusion.39) | copy-start | bytes 9437188
  117.6 12.3 %copy-start.9 = (f32[12,512,128]{1,2,0:T(8,128)S(1)}, f32[12,512,128]{1,2,0:T(8,128)}, u32[]{:S(2)}) copy-start(f32[12,512,128]{1,2,0:T(8,128)} %copy.56) | copy-start | bytes 9437188
  142.5 97.7 %all-to-all-start.1 = ((f32[12,512,128]{2,0,1:T(8,128)}), f32[12,512,128]{2,0,1:T(8,128)}, u32[]{:S(2)}, u32[]{:S(2)}) async-start(f32[12,512,128]{2,0,1:T(8,128)} %copy.59), calls=%async_computation.1 | async-start | bytes 8388608 | tf_op jit(solution)/shard_map/all_to_all | solution.py:94
  157.0 4.5 collective-permute-start.1
  161.2 3.2 collective-permute-start
  240.1 3.3 copy-start.2
  240.1 4.1 copy-start.7
  262.1 74.7 %copy-start.3 = (f32[192,32,128]{2,1,0:T(8,128)}, f32[192,32,128]{2,1,0:T(8,128)S(1)}, u32[]{:S(2)}) copy-start(f32[192,32,128]{2,1,0:T(8,128)S(1)} %get-tuple-element.6) | copy-start | bytes 9437188
  337.2 1.7 copy-start.5
  368.8 97.6 %all-to-all-start.3 = ((f32[12,512,128]{2,0,1:T(8,128)}), f32[12,512,128]{2,0,1:T(8,128)}, u32[]{:S(2)}, u32[]{:S(2)}) async-start(f32[12,512,128]{2,0,1:T(8,128)} %copy.72), calls=%async_computation.3 | async-start | bytes 8388608 | tf_op jit(solution)/shard_map/all_to_all | solution.py:94
  383.3 4.5 collective-permute-start.3
  387.5 3.2 collective-permute-start.2
  466.5 3.3 copy-start.4
  466.5 4.1 copy-start.8
where the time goes:
time: 487 us; the launch traced here: 483 us
  blocking collectives  151 us (31%)
  waiting for transfers between devices  133 us (27%)
  other arithmetic  78.5 us (16%)
  local copies, waits for them, and re-layouts  65 us (13%)
  matrix products  41 us (8%)
  starting transfers between devices  13.5 us (3%)
    all_to_all x2, blocking collectives, rate(): lax.all_to_all(thermal_estimate, 'wall', split_axis=0, concat_axis=1, til...  151 us
    all_to_all x2, waiting for transfers between devices, rate(): lax.all_to_all(boundary_operator(inner), 'wall', split_axis=1, concat_axi...  132 us
    dot_general x4, matrix products, boundary_operator(): jnp.einsum('ij,pjz->piz', wall_matrix, pencil, precision=lax.Precision.HI...  41 us
    add x2, other arithmetic, invert_heat_content(): return interval_lower_edge + offset_temp  26.4 us
    reduce_sum x1, other arithmetic, lookup(): jnp.sum(jnp.where(interval_index[None] == indices, shaped, jnp.zeros_like...  26.3 us
    slice x4, local copies, waits for them, and re-layouts, padded(): lax.slice_in_dim(block, 0, width, axis=dim)  18.6 us
    add x2, other arithmetic, heat_conductance(): return 0.5 + 1.0 / (1.0 + thermal_estimate * thermal_estimate)  14.1 us
    add x1, other arithmetic, on_device(): section + time_step * (gamma_two * second_rate + zeta_two * first_rate)  11.8 us
  transfers between devices with their start and end apart: 6, of which 4 were waited for; matrix products, arithmetic and copies ran while one was open for 10% of the time, Pallas kernels for 0%

commit v1 on v0

v1 whole, which is shorter than its diff:
```python
import functools

import jax
import jax.numpy as jnp
from jax import lax
from jax.experimental import pallas as pl
from jax.experimental.pallas import tpu as pltpu
from jax.sharding import PartitionSpec as P

NEWTON = 4

time_step = 0.4
gamma_one = 8.0 / 15.0
gamma_two = 5.0 / 12.0
zeta_two = -17.0 / 60.0

F32 = jnp.float32
BF16 = jnp.bfloat16
VMEM_BYTES = 48 * 1024 * 1024


def inverse(x):
    r = pl.reciprocal(x, approx=True)
    return r * (2.0 - x * r)


def lookup(row, index):
    return jnp.take_along_axis(jnp.broadcast_to(row, index.shape), index, axis=1)


def temperature(entries, index, tables):
    base = lookup(tables[0:1], index)
    shift = lookup(tables[1:2], index)
    first = lookup(tables[2:3], index)
    third = lookup(tables[3:4], index)
    remainder = entries - shift
    t = remainder * inverse(first)
    for _ in range(NEWTON):
        u = third * (t * t)
        t = (2.0 * u * t + remainder) * inverse(first + 3.0 * u)
    return base + t


def conductance(t):
    return 0.5 + inverse(1.0 + t * t)


def edge_rows(t):
    lanes = t.shape[1]
    r = lax.broadcasted_iota(jnp.int32, (8, lanes), 0)
    c = lax.broadcasted_iota(jnp.int32, (8, lanes), 1)
    pick = ((r == 0) & (c == 0)) | ((r == 1) & (c == lanes - 1))
    return lax.dot_general(
        pick.astype(F32), t, (((1,), (1,)), ((), ())),
        precision=lax.Precision.HIGHEST, preferred_element_type=F32,
    )


def edge_lanes(rows, lanes):
    r = lax.broadcasted_iota(jnp.int32, (8, lanes), 0)
    c = lax.broadcasted_iota(jnp.int32, (8, lanes), 1)
    put = ((r == 0) & (c == lanes - 1)) | ((r == 1) & (c == 0))
    return lax.dot_general(
        rows, put.astype(F32), (((0,), (0,)), ((), ())),
        precision=lax.Precision.HIGHEST, preferred_element_type=F32,
    )


def span_term(t, halo):
    lanes = t.shape[1]
    lane = lax.broadcasted_iota(jnp.int32, t.shape, 1)
    edge = edge_lanes(halo, lanes)
    c = conductance(t)
    c_edge = conductance(edge)
    low_t = jnp.where(lane == 0, edge, pltpu.roll(t, 1, 1))
    low_c = jnp.where(lane == 0, c_edge, pltpu.roll(c, 1, 1))
    high_t = jnp.where(lane == lanes - 1, edge, pltpu.roll(t, lanes - 1, 1))
    high_c = jnp.where(lane == lanes - 1, c_edge, pltpu.roll(c, lanes - 1, 1))
    return 0.5 * ((c + high_c) * (high_t - t) - (low_c + c) * (t - low_t))


def flat(ref):
    x = ref[...]
    return x.reshape(-1, x.shape[-1])


def first_kernel(h_ref, s_ref, tab_ref, t_ref, e_ref):
    t = temperature(flat(h_ref), flat(s_ref), tab_ref[...])
    t_ref[...] = t.reshape(t_ref.shape)
    e_ref[...] = edge_rows(t)


def middle_kernel(h_ref, s_ref, tab_ref, t_ref, halo_ref, wall_ref, t2_ref, part_ref, e_ref):
    h = flat(h_ref)
    rate = flat(wall_ref) + span_term(flat(t_ref), halo_ref[...])
    section = h + (time_step * gamma_one) * rate
    part = h + (time_step * (gamma_one + zeta_two)) * rate
    t2 = temperature(section, flat(s_ref), tab_ref[...])
    t2_ref[...] = t2.reshape(t2_ref.shape)
    part_ref[...] = part.reshape(part_ref.shape)
    e_ref[...] = edge_rows(t2)


def last_kernel(t_ref, halo_ref, wall_ref, part_ref, *refs):
    out_ref, state_ref = refs[-2:]
    t = flat(t_ref)
    rate = flat(wall_ref) + span_term(t, halo_ref[...])
    out = flat(part_ref) + (time_step * gamma_two) * rate
    out_ref[...] = out.reshape(out_ref.shape)
    state_ref[...] = t.reshape(state_ref.shape)


def split(x):
    hi = lax.reduce_precision(x, 8, 7).astype(BF16)
    return hi, (x - hi.astype(F32)).astype(BF16)


def apply_wall(hi, lo, x):
    x_hi, x_lo = split(x)
    dot = functools.partial(jnp.dot, preferred_element_type=F32)
    return dot(hi, x_hi) + (dot(hi, x_lo) + dot(lo, x_hi))


def wall_kernel(hi_ref, lo_ref, t_ref, out_ref):
    n, m, r, z = t_ref.shape
    hi, lo = hi_ref[...], lo_ref[...]
    step = 2 if m % 2 == 0 else 1
    for p in range(0, m, step):
        t = jnp.concatenate([t_ref[:, q].reshape(n * r, z) for q in range(p, p + step)], axis=1)
        g = apply_wall(hi, lo, t)
        w = apply_wall(hi, lo, conductance(t) * g)
        for q in range(step):
            out_ref[:, p + q] = w[:, q * z:(q + 1) * z].reshape(n, r, z)


def params():
    return pltpu.CompilerParams(vmem_limit_bytes=VMEM_BYTES)


def on_device(heat_content, interval_index, wall_matrix, base_temp, enth_offset, slope, curvature):
    planes, r, z = heat_content.shape
    n = lax.axis_size("wall")
    spans = lax.axis_size("span")
    own = planes // n
    chunks = next(k for k in (2, 3, 1) if own % k == 0)
    m = own // chunks
    h = heat_content.reshape(n, own, r, z)
    s = interval_index.reshape(n, own, r, z)
    tables = jnp.stack([base_temp, enth_offset, slope, curvature])
    tables = jnp.pad(tables, ((0, 4), (0, z - tables.shape[1])))
    w_hi, w_lo = split(wall_matrix)

    steps = next(k for k in (4, 2, 1) if n % k == 0 and (k == 1 or (n // k * m * r) % 128 == 0))
    nb = n // steps
    rows = nb * m * r
    piece = jax.ShapeDtypeStruct((n, m, r, z), F32)
    full = jax.ShapeDtypeStruct((n, own, r, z), F32)
    edges = jax.ShapeDtypeStruct((8, n * m * r), F32)
    whole_spec = lambda c: pl.BlockSpec((nb, m, r, z), lambda i: (i, c, 0, 0))
    piece_spec = pl.BlockSpec((nb, m, r, z), lambda i: (i, 0, 0, 0))
    edge_spec = pl.BlockSpec((8, rows), lambda i: (0, i))
    table_spec = pl.BlockSpec(tables.shape, lambda i: (0, 0))
    cells = n * m * r * z

    def cost(ops, arrays, flops=0):
        return pl.CostEstimate(flops=cells * ops + flops, bytes_accessed=cells * 4 * arrays, transcendentals=0)

    def first(c):
        return pl.pallas_call(
            first_kernel, grid=(steps,),
            in_specs=[whole_spec(c), whole_spec(c), table_spec],
            out_specs=[piece_spec, edge_spec], out_shape=[piece, edges],
            compiler_params=params(), cost_estimate=cost(100, 3), name="first",
        )(h, s, tables)

    def middle(c, t, halo, wall):
        return pl.pallas_call(
            middle_kernel, grid=(steps,),
            in_specs=[whole_spec(c), whole_spec(c), table_spec, piece_spec, edge_spec, piece_spec],
            out_specs=[piece_spec, piece_spec, edge_spec], out_shape=[piece, piece, edges],
            compiler_params=params(), cost_estimate=cost(140, 6), name="middle",
        )(h, s, tables, t, halo, wall)

    def last(c, t, halo, wall, part, outs):
        return pl.pallas_call(
            last_kernel, grid=(steps,),
            in_specs=[piece_spec, edge_spec, piece_spec, piece_spec] + [pl.BlockSpec(memory_space=pl.ANY)] * len(outs),
            out_specs=[whole_spec(c), whole_spec(c)], out_shape=[full, full],
            input_output_aliases={4 + i: i for i in range(len(outs))},
            compiler_params=params(), cost_estimate=cost(40, 5), name="last",
        )(t, halo, wall, part, *outs)

    def wall_operator(t):
        return pl.pallas_call(
            wall_kernel, out_shape=piece,
            in_specs=[pl.BlockSpec(memory_space=pltpu.VMEM)] * 3,
            out_specs=pl.BlockSpec(memory_space=pltpu.VMEM),
            compiler_params=params(), cost_estimate=cost(20, 3, 12 * n * r * cells), name="wall",
        )(w_hi, w_lo, t)

    def exchange(x):
        return lax.all_to_all(x, "wall", split_axis=0, concat_axis=0, tiled=True)

    def neighbours(e):
        forward = [(i, (i + 1) % spans) for i in range(spans)]
        if spans == 2:
            return lax.ppermute(e, "span", forward)
        backward = [(target, source) for source, target in forward]
        up = lax.ppermute(e[0:1], "span", backward)
        down = lax.ppermute(e[1:2], "span", forward)
        return jnp.concatenate([up, down, jnp.zeros_like(e[2:])], axis=0)

    parts, outs = [], ()
    started = [first(c) for c in range(chunks)]
    state = []
    for t, e in started:
        state.append((t, neighbours(e), exchange(t)))
    state = [(t, halo, exchange(wall_operator(g))) for t, halo, g in state]
    nxt = []
    for c, (t, halo, w) in enumerate(state):
        t2, part, e2 = middle(c, t, halo, w)
        nxt.append((t2, part, neighbours(e2), exchange(t2)))
    nxt = [(t, part, halo, exchange(wall_operator(g))) for t, part, halo, g in nxt]
    for c, (t, part, halo, w) in enumerate(nxt):
        outs = last(c, t, halo, w, part, outs)
    return outs[0].reshape(planes, r, z), outs[1].reshape(planes, r, z)


def solution(mesh):
    in_specs = (P(None, "wall", "span"), P(None, "wall", "span"), P(), P(), P(), P(), P())
    out_specs = (P(None, "wall", "span"), P(None, "wall", "span"))
    return jax.shard_map(
        on_device, mesh=mesh, in_specs=in_specs, out_specs=out_specs, check_vma=False
    )
```

time: 487 us -> 351 us (0.72)
  blocking collectives: 151 us -> 0 us
  waiting for transfers between devices: 133 us -> 218 us
  other arithmetic: 78.5 us -> 2.09 us
  Pallas kernels: 0 us -> 67.7 us
  local copies, waits for them, and re-layouts: 65 us -> 15.9 us
  matrix products: 41 us -> 0 us
  starting transfers between devices: 13.5 us -> 45.3 us
    all_to_all x2 -> x0, blocking collectives: 151 us -> none  [rate(): lax.all_to_all(thermal_estimate, 'wall', split_axis=0, concat_axis=1, til...]
    all_to_all x2 -> x8, waiting for transfers between devices: 132 us -> 210 us  [exchange(): return lax.all_to_all(x, 'wall', split_axis=0, concat_axis=0, tiled=True)]
    pallas_call x0 -> x10, Pallas kernels: none -> 67.7 us  [the longest x2 22 us: middle(): pl.pallas_call(middle_kernel, grid=(steps,), in_specs=[whole_spec(c), who...]
    add x5 -> x0, other arithmetic: 52.2 us -> none  [the longest x2 26.4 us: invert_heat_content(): return interval_lower_edge + offset_temp]
    dot_general x4 -> x0, matrix products: 41 us -> none  [boundary_operator(): jnp.einsum('ij,pjz->piz', wall_matrix, pencil, precision=lax.Precision.HI...]
    all_to_all x2 -> x8, starting transfers between devices: 10.4 us -> 41.3 us  [exchange(): return lax.all_to_all(x, 'wall', split_axis=0, concat_axis=0, tiled=True)]
    reduce_sum x1 -> x0, other arithmetic: 26.3 us -> none  [lookup(): jnp.sum(jnp.where(interval_index[None] == indices, shaped, jnp.zeros_like...]
    slice x6 -> x0, local copies, waits for them, and re-layouts: 24.4 us -> none  [the longest x4 18.6 us: padded(): lax.slice_in_dim(block, 0, width, axis=dim)]
  transfers between devices with their start and end apart: 6 -> 12, of which waited for: 4 -> 11; matrix products, arithmetic and copies ran while one was open for 10% -> 0% of each run, Pallas kernels for 0% -> 16%
where the time goes in v1:
time: 351 us; the launch traced here: 350 us
  waiting for transfers between devices  218 us (62%)
  Pallas kernels  67.7 us (19%)
  starting transfers between devices  45.3 us (13%)
  local copies, waits for them, and re-layouts  15.9 us (5%)
    all_to_all x8, waiting for transfers between devices, exchange(): return lax.all_to_all(x, 'wall', split_axis=0, concat_axis=0, tiled=True)  210 us
    all_to_all x8, starting transfers between devices, exchange(): return lax.all_to_all(x, 'wall', split_axis=0, concat_axis=0, tiled=True)  41.3 us
    pallas_call x2, Pallas kernels, middle(): pl.pallas_call(middle_kernel, grid=(steps,), in_specs=[whole_spec(c), who...  22 us
    pallas_call x4, Pallas kernels, wall_operator(): pl.pallas_call(wall_kernel, out_shape=piece, in_specs=[pl.BlockSpec(memor...  19.8 us
    unnamed x36, local copies, waits for them, and re-layouts  15.9 us
    pallas_call x2, Pallas kernels, first(): pl.pallas_call(first_kernel, grid=(steps,), in_specs=[whole_spec(c), whol...  14.5 us
    pallas_call x2, Pallas kernels, last(): pl.pallas_call(last_kernel, grid=(steps,), in_specs=[piece_spec, edge_spe...  11.4 us
    ppermute x4, waiting for transfers between devices, neighbours(): return lax.ppermute(e, 'span', forward)  8.22 us
  transfers between devices with their start and end apart: 12, of which 11 were waited for; matrix products, arithmetic and copies ran while one was open for 0% of the time, Pallas kernels for 16%

profile of v1, /device:TPU:11, one launch (start us, length us, event | category | flops | bytes accessed | tf_op | source)
XLA Modules:
  0.0 349.9 jit_solution(3785677568150367845)
XLA Ops:
  3.2 7.3 %first.3 = (f32[16,6,32,128]{3,2,1,0:T(8,128)S(1)}, f32[8,3072]{1,0:T(8,128)S(1)}) custom-call(f32[16,12,32,128]{3,2,1,0:T(8,128)S(1)} %bitcast.10, s32[16,12,32,128]{3,2,1,0:T(8,128)} %bitcast.12, f32[8,128]{1,0:T(8,128)S(1)} %select_maximum_fusion.tab_ref), custom_call_target="tpu_custom_call" | custom-call | flops 39321600 | bytes 4718592 | tf_op jit(solution)/shard_map/first/pallas_call | solution.py:169
  11.7 6.8 %all-to-all-start.4 = ((f32[16,6,32,128]{3,2,1,0:T(8,128)}), f32[16,6,32,128]{3,2,1,0:T(8,128)}, u32[]{:S(2)}, u32[]{:S(2)}) async-start(f32[16,6,32,128]{3,2,1,0:T(8,128)} %copy-done.4), calls=%async_computation.4 | async-start | bytes 3145728 | tf_op jit(solution)/shard_map/all_to_all | solution.py:202
  18.5 7.3 %first.2 = (f32[16,6,32,128]{3,2,1,0:T(8,128)S(1)}, f32[8,3072]{1,0:T(8,128)S(1)}) custom-call(f32[16,12,32,128]{3,2,1,0:T(8,128)S(1)} %bitcast.11, s32[16,12,32,128]{3,2,1,0:T(8,128)} %bitcast.13, f32[8,128]{1,0:T(8,128)S(1)} %select_maximum_fusion.tab_ref), custom_call_target="tpu_custom_call" | custom-call | flops 39321600 | bytes 4718592 | tf_op jit(solution)/shard_map/first/pallas_call | solution.py:169
  27.0 27.8 %all-to-all-done.4.t_ref = f32[16,6,32,128]{3,2,1,0:T(8,128)} async-done(((f32[16,6,32,128]{3,2,1,0:T(8,128)}), f32[16,6,32,128]{3,2,1,0:T(8,128)}, u32[]{:S(2)}, u32[]{:S(2)}) %all-to-all-start.4) | async-done | bytes 1572896 | tf_op jit(solution)/shard_map/all_to_all | solution.py:202
  54.8 4.9 %all-to-all-start = ((f32[16,6,32,128]{3,2,1,0:T(8,128)}), f32[16,6,32,128]{3,2,1,0:T(8,128)S(1)}, u32[]{:S(2)}, u32[]{:S(2)}) async-start(f32[16,6,32,128]{3,2,1,0:T(8,128)} %copy-done.2), calls=%async_computation | async-start | bytes 3145728 | tf_op jit(solution)/shard_map/all_to_all | solution.py:202
  61.1 6.9 %wall.6 = f32[16,6,32,128]{3,2,1,0:T(8,128)} custom-call(bf16[512,512]{1,0:T(8,128)(2,1)S(1)} %get-tuple-element.31.hi_ref, bf16[512,512]{1,0:T(8,128)(2,1)S(1)} %get-tuple-element.30.lo_ref, f32[16,6,32,128]{3,2,1,0:T(8,128)} %all-to-all-done.4.t_ref), custom_call_target="tpu_custom_call" | custom-call | flops 2423783424 | bytes 4718592 | tf_op jit(solution)/shard_map/wall/pallas_call | solution.py:194
  68.0 27.9 %all-to-all-done.t_ref = f32[16,6,32,128]{3,2,1,0:T(8,128)S(1)} async-done(((f32[16,6,32,128]{3,2,1,0:T(8,128)}), f32[16,6,32,128]{3,2,1,0:T(8,128)S(1)}, u32[]{:S(2)}, u32[]{:S(2)}) %all-to-all-start) | async-done | bytes 1572896 | tf_op jit(solution)/shard_map/all_to_all | solution.py:202
  95.9 4.9 %all-to-all-start.5 = ((f32[16,6,32,128]{3,2,1,0:T(8,128)}), f32[16,6,32,128]{3,2,1,0:T(8,128)}, u32[]{:S(2)}, u32[]{:S(2)}) async-start(f32[16,6,32,128]{3,2,1,0:T(8,128)} %wall.6), calls=%async_computation.5 | async-start | bytes 3145728 | tf_op jit(solution)/shard_map/all_to_all | solution.py:202
  100.8 5.1 %wall.4 = f32[16,6,32,128]{3,2,1,0:T(8,128)} custom-call(bf16[512,512]{1,0:T(8,128)(2,1)S(1)} %get-tuple-element.31.hi_ref, bf16[512,512]{1,0:T(8,128)(2,1)S(1)} %get-tuple-element.30.lo_ref, f32[16,6,32,128]{3,2,1,0:T(8,128)S(1)} %all-to-all-done.t_ref), custom_call_target="tpu_custom_call" | custom-call | flops 2423783424 | bytes 4718592 | tf_op jit(solution)/shard_map/wall/pallas_call | solution.py:194
  105.9 31.2 %all-to-all-done.5.wall_ref = f32[16,6,32,128]{3,2,1,0:T(8,128)} async-done(((f32[16,6,32,128]{3,2,1,0:T(8,128)}), f32[16,6,32,128]{3,2,1,0:T(8,128)}, u32[]{:S(2)}, u32[]{:S(2)}) %all-to-all-start.5) | async-done | bytes 1572896 | tf_op jit(solution)/shard_map/all_to_all | solution.py:202
  137.1 4.9 %all-to-all-start.1 = ((f32[16,6,32,128]{3,2,1,0:T(8,128)}), f32[16,6,32,128]{3,2,1,0:T(8,128)}, u32[]{:S(2)}, u32[]{:S(2)}) async-start(f32[16,6,32,128]{3,2,1,0:T(8,128)} %wall.4), calls=%async_computation.1 | async-start | bytes 3145728 | tf_op jit(solution)/shard_map/all_to_all | solution.py:202
  146.2 11.0 %middle.3 = (f32[16,6,32,128]{3,2,1,0:T(8,128)}, f32[16,6,32,128]{3,2,1,0:T(8,128)S(1)}, f32[8,3072]{1,0:T(8,128)S(1)}) custom-call(f32[16,12,32,128]{3,2,1,0:T(8,128)} %bitcast.8, s32[16,12,32,128]{3,2,1,0:T(8,128)} %bitcast.14, f32[8,128]{1,0:T(8,128)S(1)} %select_maximum_fusion.tab_ref, f32[16,6,32,128]{3,2,1,0:T(8,128)S(1)} %copy-done.5, ...), custom_call_target="tpu_custom_call" | custom-call | flops 55050240 | bytes 9437184 | tf_op jit(solution)/shard_map/middle/pallas_call | solution.py:177
  158.4 19.9 %all-to-all-done.1.wall_ref = f32[16,6,32,128]{3,2,1,0:T(8,128)} async-done(((f32[16,6,32,128]{3,2,1,0:T(8,128)}), f32[16,6,32,128]{3,2,1,0:T(8,128)}, u32[]{:S(2)}, u32[]{:S(2)}) %all-to-all-start.1) | async-done | bytes 1572896 | tf_op jit(solution)/shard_map/all_to_all | solution.py:202
  178.3 5.0 %all-to-all-start.6 = ((f32[16,6,32,128]{3,2,1,0:T(8,128)}), f32[16,6,32,128]{3,2,1,0:T(8,128)S(1)}, u32[]{:S(2)}, u32[]{:S(2)}) async-start(f32[16,6,32,128]{3,2,1,0:T(8,128)} %get-tuple-element.23.t_ref), calls=%async_computation.6 | async-start | bytes 3145728 | tf_op jit(solution)/shard_map/all_to_all | solution.py:202
  187.4 11.0 %middle.2 = (f32[16,6,32,128]{3,2,1,0:T(8,128)}, f32[16,6,32,128]{3,2,1,0:T(8,128)S(1)}, f32[8,3072]{1,0:T(8,128)S(1)}) custom-call(f32[16,12,32,128]{3,2,1,0:T(8,128)} %bitcast.9, s32[16,12,32,128]{3,2,1,0:T(8,128)} %bitcast.15, f32[8,128]{1,0:T(8,128)S(1)} %select_maximum_fusion.tab_ref, f32[16,6,32,128]{3,2,1,0:T(8,128)S(1)} %copy-done.3, ...), custom_call_target="tpu_custom_call" | custom-call | flops 55050240 | bytes 9437184 | tf_op jit(solution)/shard_map/middle/pallas_call | solution.py:177
  199.5 20.0 %all-to-all-done.6.t_ref = f32[16,6,32,128]{3,2,1,0:T(8,128)S(1)} async-done(((f32[16,6,32,128]{3,2,1,0:T(8,128)}), f32[16,6,32,128]{3,2,1,0:T(8,128)S(1)}, u32[]{:S(2)}, u32[]{:S(2)}) %all-to-all-start.6) | async-done | bytes 1572896 | tf_op jit(solution)/shard_map/all_to_all | solution.py:202
  219.5 4.9 %all-to-all-start.2 = ((f32[16,6,32,128]{3,2,1,0:T(8,128)}), f32[16,6,32,128]{3,2,1,0:T(8,128)S(1)}, u32[]{:S(2)}, u32[]{:S(2)}) async-start(f32[16,6,32,128]{3,2,1,0:T(8,128)} %get-tuple-element.18.t_ref), calls=%async_computation.2 | async-start | bytes 3145728 | tf_op jit(solution)/shard_map/all_to_all | solution.py:202
  231.6 29.0 %all-to-all-done.2.t_ref = f32[16,6,32,128]{3,2,1,0:T(8,128)S(1)} async-done(((f32[16,6,32,128]{3,2,1,0:T(8,128)}), f32[16,6,32,128]{3,2,1,0:T(8,128)S(1)}, u32[]{:S(2)}, u32[]{:S(2)}) %all-to-all-start.2) | async-done | bytes 1572896 | tf_op jit(solution)/shard_map/all_to_all | solution.py:202
  260.6 4.9 %all-to-all-start.7 = ((f32[16,6,32,128]{3,2,1,0:T(8,128)}), f32[16,6,32,128]{3,2,1,0:T(8,128)S(1)}, u32[]{:S(2)}, u32[]{:S(2)}) async-start(f32[16,6,32,128]{3,2,1,0:T(8,128)} %copy-done.7), calls=%async_computation.7 | async-start | bytes 3145728 | tf_op jit(solution)/shard_map/all_to_all | solution.py:202
  272.7 29.0 %all-to-all-done.7.wall_ref = f32[16,6,32,128]{3,2,1,0:T(8,128)S(1)} async-done(((f32[16,6,32,128]{3,2,1,0:T(8,128)}), f32[16,6,32,128]{3,2,1,0:T(8,128)S(1)}, u32[]{:S(2)}, u32[]{:S(2)}) %all-to-all-start.7) | async-done | bytes 1572896 | tf_op jit(solution)/shard_map/all_to_all | solution.py:202
  301.7 4.9 %all-to-all-start.3 = ((f32[16,6,32,128]{3,2,1,0:T(8,128)}), f32[16,6,32,128]{3,2,1,0:T(8,128)S(1)}, u32[]{:S(2)}, u32[]{:S(2)}) async-start(f32[16,6,32,128]{3,2,1,0:T(8,128)} %copy-done.6), calls=%async_computation.3 | async-start | bytes 3145728 | tf_op jit(solution)/shard_map/all_to_all | solution.py:202
  312.0 5.7 %last.2 = (f32[16,12,32,128]{3,2,1,0:T(8,128)}, f32[16,12,32,128]{3,2,1,0:T(8,128)}) custom-call(f32[16,6,32,128]{3,2,1,0:T(8,128)} %get-tuple-element.23.t_ref, f32[8,3072]{1,0:T(8,128)S(1)} %collective-permute-done.3.halo_ref, f32[16,6,32,128]{3,2,1,0:T(8,128)S(1)} %all-to-all-done.7.wall_ref, f32[16,6,32,128]{3,2,1,0:T(8,128)S(1)} %copy-done.9), custom_call_target="tpu_custom_call" | custom-call | flops 15728640 | bytes 7864320 | tf_op jit(solution)/shard_map/last/pallas_call | solution.py:185
  317.7 25.1 %all-to-all-done.3.wall_ref = f32[16,6,32,128]{3,2,1,0:T(8,128)S(1)} async-done(((f32[16,6,32,128]{3,2,1,0:T(8,128)}), f32[16,6,32,128]{3,2,1,0:T(8,128)S(1)}, u32[]{:S(2)}, u32[]{:S(2)}) %all-to-all-start.3) | async-done | bytes 1572896 | tf_op jit(solution)/shard_map/all_to_all | solution.py:202
  344.2 5.7 %last.3 = (f32[16,12,32,128]{3,2,1,0:T(8,128)}, f32[16,12,32,128]{3,2,1,0:T(8,128)}) custom-call(f32[16,6,32,128]{3,2,1,0:T(8,128)} %get-tuple-element.18.t_ref, f32[8,3072]{1,0:T(8,128)S(1)} %collective-permute-done.1.halo_ref, f32[16,6,32,128]{3,2,1,0:T(8,128)S(1)} %all-to-all-done.3.wall_ref, ...), custom_call_target="tpu_custom_call", output_to_operand_aliasing={{0}: (4, {}), {1}: (5, {})} | custom-call | flops 15728640 | bytes 7864320 | tf_op jit(solution)/shard_map/last/pallas_call | solution.py:185
  (48 shorter events, 38.1 us)
Async XLA Ops:
  1.3 1.9 copy-start
  10.5 1.2 copy-start.4
  11.7 6.8 %copy-start.1 = (f32[192,32,128]{2,1,0:T(8,128)S(1)}, f32[192,32,128]{2,1,0:T(8,128)}, u32[]{:S(2)}) copy-start(f32[192,32,128]{2,1,0:T(8,128)} %param.7) | copy-start | bytes 9437188
  11.7 43.1 %all-to-all-start.4 = ((f32[16,6,32,128]{3,2,1,0:T(8,128)}), f32[16,6,32,128]{3,2,1,0:T(8,128)}, u32[]{:S(2)}, u32[]{:S(2)}) async-start(f32[16,6,32,128]{3,2,1,0:T(8,128)} %copy-done.4), calls=%async_computation.4 | async-start | bytes 3145728 | tf_op jit(solution)/shard_map/all_to_all | solution.py:202
  25.8 1.2 copy-start.2
  54.8 41.1 %all-to-all-start = ((f32[16,6,32,128]{3,2,1,0:T(8,128)}), f32[16,6,32,128]{3,2,1,0:T(8,128)S(1)}, u32[]{:S(2)}, u32[]{:S(2)}) async-start(f32[16,6,32,128]{3,2,1,0:T(8,128)} %copy-done.2), calls=%async_computation | async-start | bytes 3145728 | tf_op jit(solution)/shard_map/all_to_all | solution.py:202
  61.1 39.7 %copy-start.12 = (bf16[512,512]{1,0:T(8,128)(2,1)}, bf16[512,512]{1,0:T(8,128)(2,1)S(1)}, u32[]{:S(2)}) copy-start(bf16[512,512]{1,0:T(8,128)(2,1)S(1)} %get-tuple-element.30.lo_ref) | copy-start | bytes 1572868
  61.1 39.7 %copy-start.15 = (bf16[512,512]{1,0:T(8,128)(2,1)}, bf16[512,512]{1,0:T(8,128)(2,1)S(1)}, u32[]{:S(2)}) copy-start(bf16[512,512]{1,0:T(8,128)(2,1)S(1)} %get-tuple-element.31.hi_ref) | copy-start | bytes 1572868
  95.9 41.2 %all-to-all-start.5 = ((f32[16,6,32,128]{3,2,1,0:T(8,128)}), f32[16,6,32,128]{3,2,1,0:T(8,128)}, u32[]{:S(2)}, u32[]{:S(2)}) async-start(f32[16,6,32,128]{3,2,1,0:T(8,128)} %wall.6), calls=%async_computation.5 | async-start | bytes 3145728 | tf_op jit(solution)/shard_map/all_to_all | solution.py:202
  105.9 40.3 %copy-start.5 = (f32[16,6,32,128]{3,2,1,0:T(8,128)S(1)}, f32[16,6,32,128]{3,2,1,0:T(8,128)}, u32[]{:S(2)}) copy-start(f32[16,6,32,128]{3,2,1,0:T(8,128)} %copy-done.4) | copy-start | bytes 4718596
  137.1 41.2 %all-to-all-start.1 = ((f32[16,6,32,128]{3,2,1,0:T(8,128)}), f32[16,6,32,128]{3,2,1,0:T(8,128)}, u32[]{:S(2)}, u32[]{:S(2)}) async-start(f32[16,6,32,128]{3,2,1,0:T(8,128)} %wall.4), calls=%async_computation.1 | async-start | bytes 3145728 | tf_op jit(solution)/shard_map/all_to_all | solution.py:202
  142.0 4.2 %collective-permute-start.2 = (f32[8,3072]{1,0:T(8,128)S(1)}, f32[8,3072]{1,0:T(8,128)S(1)}, u32[]{:S(2)}, u32[]{:S(2)}) collective-permute-start(f32[8,3072]{1,0:T(8,128)S(1)} %get-tuple-element.22), channel_id=1, source_target_pairs={{0,1},{1,0},{2,3},{3,2},{4,5},{5,4},{6,7},{7,6},{8,9},{9,8},{10,11... | collective-permute-start | bytes 294920 | tf_op jit(solution)/shard_map/ppermute | solution.py:207
  157.2 1.2 copy-start.8
  178.3 9.1 %copy-start.3 = (f32[16,6,32,128]{3,2,1,0:T(8,128)S(1)}, f32[16,6,32,128]{3,2,1,0:T(8,128)}, u32[]{:S(2)}) copy-start(f32[16,6,32,128]{3,2,1,0:T(8,128)} %copy-done.2) | copy-start | bytes 4718596
  178.3 41.2 %all-to-all-start.6 = ((f32[16,6,32,128]{3,2,1,0:T(8,128)}), f32[16,6,32,128]{3,2,1,0:T(8,128)S(1)}, u32[]{:S(2)}, u32[]{:S(2)}) async-start(f32[16,6,32,128]{3,2,1,0:T(8,128)} %get-tuple-element.23.t_ref), calls=%async_computation.6 | async-start | bytes 3145728 | tf_op jit(solution)/shard_map/all_to_all | solution.py:202
  183.3 4.0 %collective-permute-start = (f32[8,3072]{1,0:T(8,128)S(1)}, f32[8,3072]{1,0:T(8,128)S(1)}, u32[]{:S(2)}, u32[]{:S(2)}) collective-permute-start(f32[8,3072]{1,0:T(8,128)S(1)} %get-tuple-element.17), channel_id=1, source_target_pairs={{0,1},{1,0},{2,3},{3,2},{4,5},{5,4},{6,7},{7,6},{8,9},{9,8},{10,11... | collective-permute-start | bytes 294920 | tf_op jit(solution)/shard_map/ppermute | solution.py:207
  219.5 41.1 %all-to-all-start.2 = ((f32[16,6,32,128]{3,2,1,0:T(8,128)}), f32[16,6,32,128]{3,2,1,0:T(8,128)S(1)}, u32[]{:S(2)}, u32[]{:S(2)}) async-start(f32[16,6,32,128]{3,2,1,0:T(8,128)} %get-tuple-element.18.t_ref), calls=%async_computation.2 | async-start | bytes 3145728 | tf_op jit(solution)/shard_map/all_to_all | solution.py:202
  260.6 41.1 %all-to-all-start.7 = ((f32[16,6,32,128]{3,2,1,0:T(8,128)}), f32[16,6,32,128]{3,2,1,0:T(8,128)S(1)}, u32[]{:S(2)}, u32[]{:S(2)}) async-start(f32[16,6,32,128]{3,2,1,0:T(8,128)} %copy-done.7), calls=%async_computation.7 | async-start | bytes 3145728 | tf_op jit(solution)/shard_map/all_to_all | solution.py:202
  271.5 1.2 copy-start.6
  301.7 41.1 %all-to-all-start.3 = ((f32[16,6,32,128]{3,2,1,0:T(8,128)}), f32[16,6,32,128]{3,2,1,0:T(8,128)S(1)}, u32[]{:S(2)}, u32[]{:S(2)}) async-start(f32[16,6,32,128]{3,2,1,0:T(8,128)} %copy-done.6), calls=%async_computation.3 | async-start | bytes 3145728 | tf_op jit(solution)/shard_map/all_to_all | solution.py:202
  306.6 4.0 %collective-permute-start.3 = (f32[8,3072]{1,0:T(8,128)S(1)}, f32[8,3072]{1,0:T(8,128)S(1)}, u32[]{:S(2)}, u32[]{:S(2)}) collective-permute-start(f32[8,3072]{1,0:T(8,128)S(1)} %get-tuple-element.24), channel_id=1, source_target_pairs={{0,1},{1,0},{2,3},{3,2},{4,5},{5,4},{6,7},{7,6},{8,9},{9,8},{10,11... | collective-permute-start | bytes 294920 | tf_op jit(solution)/shard_map/ppermute | solution.py:207
  307.9 9.9 %collective-permute-start.1 = (f32[8,3072]{1,0:T(8,128)S(1)}, f32[8,3072]{1,0:T(8,128)S(1)}, u32[]{:S(2)}, u32[]{:S(2)}) collective-permute-start(f32[8,3072]{1,0:T(8,128)S(1)} %get-tuple-element.19), channel_id=1, source_target_pairs={{0,1},{1,0},{2,3},{3,2},{4,5},{5,4},{6,7},{7,6},{8,9},{9,8},{10,11... | collective-permute-start | bytes 294920 | tf_op jit(solution)/shard_map/ppermute | solution.py:207
  310.6 1.4 copy-start.9
  342.8 1.4 copy-start.11
  (6 other events, 6.5 us)

commit v2 on v1

v2 whole, which is shorter than its diff:
```python
import functools

import jax
import jax.numpy as jnp
from jax import lax
from jax.experimental import pallas as pl
from jax.experimental.pallas import tpu as pltpu
from jax.sharding import PartitionSpec as P

NEWTON = 4

time_step = 0.4
gamma_one = 8.0 / 15.0
gamma_two = 5.0 / 12.0
zeta_two = -17.0 / 60.0

F32 = jnp.float32
BF16 = jnp.bfloat16
VMEM_BYTES = 24 * 1024 * 1024
CHUNKS = (2, 3, 1)
ORDER = (4, 2, 7, 1, 6, 5, 3)
WINDOW = 4
EARLY = 6


def inverse(x):
    r = pl.reciprocal(x, approx=True)
    return r * (2.0 - x * r)


def lookup(row, index):
    return jnp.take_along_axis(jnp.broadcast_to(row, index.shape), index, axis=1)


def temperature(entries, index, tables):
    base = lookup(tables[0:1], index)
    shift = lookup(tables[1:2], index)
    first = lookup(tables[2:3], index)
    third = lookup(tables[3:4], index)
    remainder = entries - shift
    t = remainder * inverse(first)
    for _ in range(NEWTON):
        u = third * (t * t)
        t = (2.0 * u * t + remainder) * inverse(first + 3.0 * u)
    return base + t


def conductance(t):
    return 0.5 + inverse(1.0 + t * t)


def edge_rows(t):
    lanes = t.shape[1]
    r = lax.broadcasted_iota(jnp.int32, (8, lanes), 0)
    c = lax.broadcasted_iota(jnp.int32, (8, lanes), 1)
    pick = ((r == 0) & (c == 0)) | ((r == 1) & (c == lanes - 1))
    return lax.dot_general(
        pick.astype(F32), t, (((1,), (1,)), ((), ())),
        precision=lax.Precision.HIGHEST, preferred_element_type=F32,
    )


def edge_lanes(rows, lanes):
    r = lax.broadcasted_iota(jnp.int32, (8, lanes), 0)
    c = lax.broadcasted_iota(jnp.int32, (8, lanes), 1)
    put = ((r == 0) & (c == lanes - 1)) | ((r == 1) & (c == 0))
    return lax.dot_general(
        rows, put.astype(F32), (((0,), (0,)), ((), ())),
        precision=lax.Precision.HIGHEST, preferred_element_type=F32,
    )


def span_term(t, halo):
    lanes = t.shape[1]
    lane = lax.broadcasted_iota(jnp.int32, t.shape, 1)
    edge = edge_lanes(halo, lanes)
    c = conductance(t)
    c_edge = conductance(edge)
    low_t = jnp.where(lane == 0, edge, pltpu.roll(t, 1, 1))
    low_c = jnp.where(lane == 0, c_edge, pltpu.roll(c, 1, 1))
    high_t = jnp.where(lane == lanes - 1, edge, pltpu.roll(t, lanes - 1, 1))
    high_c = jnp.where(lane == lanes - 1, c_edge, pltpu.roll(c, lanes - 1, 1))
    return 0.5 * ((c + high_c) * (high_t - t) - (low_c + c) * (t - low_t))


def spread(ref):
    return ref[...].reshape(-1, ref.shape[-1])


def fetched(me_ref, ref):
    chip, core = me_ref[0], me_ref[1]
    return jnp.concatenate(
        [ref[chip ^ p, core ^ q, 0] for q in range(2) for p in range(ref.shape[0])], axis=0
    )


def store(same_ref, other_ref, x):
    half = x.shape[0] // 2
    same_ref[...] = x[:half].reshape(same_ref.shape)
    other_ref[...] = x[half:].reshape(other_ref.shape)


def first_kernel(me_ref, h_ref, s_ref, tab_ref, same_ref, other_ref, e_ref):
    t = temperature(fetched(me_ref, h_ref), fetched(me_ref, s_ref), tab_ref[...])
    store(same_ref, other_ref, t)
    e_ref[0] = edge_rows(t)


def rate_of(t, halo_ref, crossed_ref, back_refs):
    wall = jnp.concatenate([spread(ref) for ref in back_refs] + [spread(crossed_ref)], axis=0)
    return wall + span_term(t, halo_ref[0])


def middle_kernel(chips, me_ref, h_ref, s_ref, tab_ref, same_ref, other_ref, halo_ref, crossed_ref, *refs):
    back_refs, (same2_ref, other2_ref, part_ref, e_ref) = refs[:chips], refs[chips:]
    h = fetched(me_ref, h_ref)
    t = jnp.concatenate([spread(same_ref), spread(other_ref)], axis=0)
    rate = rate_of(t, halo_ref, crossed_ref, back_refs)
    section = h + (time_step * gamma_one) * rate
    part_ref[...] = (h + (time_step * (gamma_one + zeta_two)) * rate).reshape(part_ref.shape)
    t2 = temperature(section, fetched(me_ref, s_ref), tab_ref[...])
    store(same2_ref, other2_ref, t2)
    e_ref[0] = edge_rows(t2)


def last_kernel(chips, me_ref, same_ref, other_ref, halo_ref, part_ref, crossed_ref, *refs):
    back_refs = refs[:chips]
    out_ref, state_ref = refs[-2:]
    t = jnp.concatenate([spread(same_ref), spread(other_ref)], axis=0)
    rate = rate_of(t, halo_ref, crossed_ref, back_refs)
    out = part_ref[...].reshape(t.shape) + (time_step * gamma_two) * rate
    chip, core = me_ref[0], me_ref[1]
    r = out_ref.shape[-2]
    for q in range(2):
        for p in range(chips):
            at = (q * chips + p) * r
            out_ref[chip ^ p, core ^ q, 0] = out[at:at + r]
            state_ref[chip ^ p, core ^ q, 0] = t[at:at + r]


def pair_kernel(same_ref, crossed_ref, *outs):
    for p, out in enumerate(outs, 1):
        out[0] = same_ref[p]
        out[1] = crossed_ref[p]


def gather_kernel(*refs):
    for p, ref in enumerate(refs[:-1]):
        refs[-1][p] = ref[0]


def split(x):
    hi = lax.reduce_precision(x, 8, 7).astype(BF16)
    return hi, (x - hi.astype(F32)).astype(BF16)


def apply_wall(hi, lo, x):
    x_hi, x_lo = split(x)
    dot = functools.partial(jnp.dot, preferred_element_type=F32)
    return dot(hi, x_hi) + (dot(hi, x_lo) + dot(lo, x_hi))


def wall_kernel(chips, me_ref, hi_ref, lo_ref, same_ref, crossed_ref, *refs):
    moved, outs, hold = refs[:chips - 1], refs[chips - 1:-1], refs[-1]
    n, m, r, z = hold.shape
    chip, core = me_ref[0], me_ref[1]
    for q in range(2):
        hold[chip * 2 + (core ^ q)] = (same_ref, crossed_ref)[q][0]
        for p in range(1, chips):
            hold[(chip ^ p) * 2 + (core ^ q)] = moved[p - 1][q]
    hi, lo = hi_ref[...], lo_ref[...]
    t = jnp.concatenate([hold[:, k].reshape(n * r, z) for k in range(m)], axis=1)
    g = apply_wall(hi, lo, t)
    w = apply_wall(hi, lo, conductance(t) * g)
    for k in range(m):
        hold[:, k] = w[:, k * z:(k + 1) * z].reshape(n, r, z)
    for q in range(2):
        for p in range(chips):
            outs[p][q] = hold[(chip ^ p) * 2 + (core ^ q)]


def params():
    return pltpu.CompilerParams(vmem_limit_bytes=VMEM_BYTES)


def on_device(heat_content, interval_index, wall_matrix, base_temp, enth_offset, slope, curvature):
    planes, r, z = heat_content.shape
    n = lax.axis_size("wall")
    spans = lax.axis_size("span")
    chips = n // 2
    own = planes // n
    chunks = next(k for k in CHUNKS if own % k == 0)
    m = own // chunks
    order = ORDER if chips == 8 else list(range(1, chips))
    index = lax.axis_index("wall")
    me = jnp.stack([index // 2, index % 2]).astype(jnp.int32)
    h = heat_content.reshape(chips, 2, own, r, z)
    s = interval_index.reshape(chips, 2, own, r, z)
    tables = jnp.stack([base_temp, enth_offset, slope, curvature])
    tables = jnp.pad(tables, ((0, 4), (0, z - tables.shape[1])))
    w_hi, w_lo = split(wall_matrix)

    half = jax.ShapeDtypeStruct((chips, m, r, z), F32)
    pair = jax.ShapeDtypeStruct((2, m, r, z), F32)
    both = jax.ShapeDtypeStruct((2, chips, m, r, z), F32)
    full = jax.ShapeDtypeStruct((chips, 2, own, r, z), F32)
    edges = jax.ShapeDtypeStruct((m, 8, n * r), F32)
    whole_spec = lambda c: pl.BlockSpec((chips, 2, 1, r, z), lambda i, me: (0, 0, c * m + i, 0, 0))
    half_spec = pl.BlockSpec((chips, 1, r, z), lambda i, me: (0, i, 0, 0))
    back_spec = pl.BlockSpec((1, 1, r, z), lambda i, me: (0, i, 0, 0))
    both_spec = pl.BlockSpec((2, chips, 1, r, z), lambda i, me: (0, 0, i, 0, 0))
    edge_spec = pl.BlockSpec((1, 8, n * r), lambda i, me: (i, 0, 0))
    table_spec = pl.BlockSpec(tables.shape, lambda i, me: (0, 0))
    hbm = pl.BlockSpec(memory_space=pl.ANY)
    cells = n * m * r * z

    def cost(ops, arrays, flops=0):
        return pl.CostEstimate(flops=cells * ops + flops, bytes_accessed=cells * 4 * arrays, transcendentals=0)

    def call(kernel, ins, outs, shapes, estimate, name, aliases={}, scratch=(), steps=m):
        grid = pltpu.PrefetchScalarGridSpec(
            num_scalar_prefetch=1, grid=(steps,), in_specs=ins, out_specs=outs, scratch_shapes=scratch
        )
        return pl.pallas_call(
            kernel, grid_spec=grid, out_shape=shapes, input_output_aliases=aliases,
            compiler_params=params(), cost_estimate=estimate, name=name,
        )

    def first(c, me):
        return call(
            first_kernel, [whole_spec(c), whole_spec(c), table_spec], [half_spec, half_spec, edge_spec],
            [half, half, edges], cost(100, 3), "first",
        )(me, h, s, tables)

    def middle(c, same, other, halo, crossed, back):
        return call(
            functools.partial(middle_kernel, chips),
            [whole_spec(c), whole_spec(c), table_spec, half_spec, half_spec, edge_spec, half_spec] + [back_spec] * chips,
            [half_spec, half_spec, both_spec, edge_spec], [half, half, both, edges], cost(140, 6), "middle",
        )(me, h, s, tables, same, other, halo, crossed, *back)

    def last(c, same, other, halo, part, crossed, back, outs):
        return call(
            functools.partial(last_kernel, chips),
            [half_spec, half_spec, edge_spec, both_spec, half_spec] + [back_spec] * chips + [hbm] * len(outs),
            [whole_spec(c)] * 2, [full] * 2, cost(40, 5), "last",
            {6 + chips + i: i for i in range(len(outs))},
        )(me, same, other, halo, part, crossed, *back, *outs)

    def block(shape, at=0):
        return pl.BlockSpec(shape, lambda i, me: (at,) + (0,) * (len(shape) - 1))

    def wall_operator(same, crossed, moved):
        return call(
            functools.partial(wall_kernel, chips),
            [block(w_hi.shape)] * 2 + [block((1, m, r, z))] * 2 + [block(pair.shape)] * (chips - 1),
            [block(pair.shape)] * chips, [pair] * chips, cost(20, 3, 12 * n * r * cells), "wall",
            scratch=[pltpu.VMEM((n, m, r, z), F32)], steps=1,
        )(me, w_hi, w_lo, same, crossed, *moved)

    def pairs(same, crossed):
        vmem = pl.BlockSpec(memory_space=pltpu.VMEM)
        return pl.pallas_call(
            pair_kernel, out_shape=[pair] * (chips - 1), in_specs=[vmem] * 2, out_specs=[vmem] * (chips - 1),
            compiler_params=params(), cost_estimate=cost(1, 2), name="pairs",
        )(same, crossed)

    def gather(back):
        return pl.pallas_call(
            gather_kernel, grid=(1,), out_shape=half,
            in_specs=[pl.BlockSpec((1, m, r, z), lambda i: (1, 0, 0, 0))] * chips,
            out_specs=pl.BlockSpec(half.shape, lambda i: (0, 0, 0, 0)),
            compiler_params=params(), cost_estimate=cost(1, 1), name="gather",
        )(*back)

    sent = []

    def after(x, tokens):
        return lax.optimization_barrier((x, *tokens))[0] if tokens else x

    def between_chips(arrays, places, tokens=()):
        moved = {}
        for p in (order[k] for k in places):
            x = after(arrays[p - 1], tuple(sent[-WINDOW:][:1] if len(sent) >= WINDOW else ()) + tuple(tokens))
            moved[p] = lax.ppermute(x, "wall", [(i, i ^ (2 * p)) for i in range(n)])
            sent.append(moved[p])
            tokens = ()
        return moved

    def between_cores(x):
        return lax.ppermute(x, "wall", [(i, i ^ 1) for i in range(n)])

    def neighbours(e):
        forward = [(i, (i + 1) % spans) for i in range(spans)]
        if spans == 2:
            return lax.ppermute(e, "span", forward)
        backward = [(target, source) for source, target in forward]
        up = lax.ppermute(e[:, 0:1], "span", backward)
        down = lax.ppermute(e[:, 1:2], "span", forward)
        return jnp.concatenate([up, down, jnp.zeros_like(e[:, 2:])], axis=1)

    chunk = [dict() for _ in range(chunks)]
    outs = ()

    def start_first(c, tokens):
        d = chunk[c]
        d["same"], d["other"], e = first(c, after(me, tokens))
        d["crossed"] = between_cores(d["other"])
        d["halo"] = neighbours(e)
        d["send"] = pairs(d["same"], d["crossed"])
        return d["same"]

    def produce(c, phase, tokens=()):
        nonlocal outs
        d = chunk[c]
        moved = [d["moved"][p] for p in range(1, chips)]
        if phase in (1, 3):
            w = wall_operator(d["same"], after(d["crossed"], tokens), moved)
            d["own"], d["send"] = w[0], w[1:]
            return w[0]
        back = [d["own"]] + moved
        crossed = after(between_cores(gather(back)), tokens)
        if phase == 2:
            d["same"], d["other"], d["part"], e = middle(c, d["same"], d["other"], d["halo"], crossed, back)
            d["crossed"] = between_cores(d["other"])
            d["halo"] = neighbours(e)
            d["send"] = pairs(d["same"], d["crossed"])
            return d["same"]
        outs = last(c, d["same"], d["other"], d["halo"], d["part"], crossed, back, outs)
        return outs[0]

    start_first(0, ())
    early = min(EARLY, len(order))
    for j in range(4 * chunks):
        phase, c = divmod(j, chunks)
        d = chunk[c]
        tokens = []
        d["moved"] = between_chips(d["send"], range(early))
        if j + 1 < chunks:
            tokens.append(start_first(j + 1, (d["send"][order[0] - 1],)))
        if j >= 1:
            before, k = divmod(j - 1, chunks)
            tokens.append(produce(k, before + 1))
        late = list(range(early, len(order)))
        d["moved"].update(between_chips(d["send"], late[:-1], tokens))
        d["moved"].update(between_chips(d["send"], late[-1:], (d["halo"],) if phase in (0, 2) else ()))
    produce(chunks - 1, 4)
    return outs[0].reshape(planes, r, z), outs[1].reshape(planes, r, z)


def solution(mesh):
    in_specs = (P(None, "wall", "span"), P(None, "wall", "span"), P(), P(), P(), P(), P())
    out_specs = (P(None, "wall", "span"), P(None, "wall", "span"))
    return jax.shard_map(
        on_device, mesh=mesh, in_specs=in_specs, out_specs=out_specs, check_vma=False
    )
```

time: 351 us -> 345 us (0.983)
  waiting for transfers between devices: 218 us -> 165 us
  starting transfers between devices: 45.3 us -> 97.8 us
  local copies, waits for them, and re-layouts: 15.9 us -> 3.79 us
  Pallas kernels: 67.7 us -> 73.7 us
    all_to_all x8 -> x0, waiting for transfers between devices: 210 us -> none  [exchange(): return lax.all_to_all(x, 'wall', split_axis=0, concat_axis=0, tiled=True)]
    ppermute x0 -> x64, waiting for transfers between devices: none -> 165 us  [the longest x56 163 us: between_chips(): moved[p] = lax.ppermute(x, 'wall', [(i, i ^ 2 * p) for i in range(n)])]
    ppermute x0 -> x64, starting transfers between devices: none -> 93.3 us  [the longest x56 82 us: between_chips(): moved[p] = lax.ppermute(x, 'wall', [(i, i ^ 2 * p) for i in range(n)])]
    all_to_all x8 -> x0, starting transfers between devices: 41.3 us -> none  [exchange(): return lax.all_to_all(x, 'wall', split_axis=0, concat_axis=0, tiled=True)]
    unnamed x36 -> x10, local copies, waits for them, and re-layouts: 15.9 us -> 3.79 us
    ppermute x4, waiting for transfers between devices: 8.22 us -> 0.01 us  [neighbours(): return lax.ppermute(e, 'span', forward)]
    pallas_call x10 -> x18, Pallas kernels: 67.7 us -> 73.7 us  [the longest x2 23.7 us: middle(): call(functools.partial(middle_kernel, chips), [whole_spec(c), whole_spec(...]
  transfers between devices with their start and end apart: 12 -> 68, of which waited for: 11 -> 29; matrix products, arithmetic and copies ran while one was open for 0% -> 0% of each run, Pallas kernels for 16% -> 15%
where the time goes in v2:
time: 345 us; the launch traced here: 342 us
  waiting for transfers between devices  165 us (48%)
  starting transfers between devices  97.8 us (28%)
  Pallas kernels  73.7 us (21%)
  local copies, waits for them, and re-layouts  3.79 us (1%)
    ppermute x56, waiting for transfers between devices, between_chips(): moved[p] = lax.ppermute(x, 'wall', [(i, i ^ 2 * p) for i in range(n)])  163 us
    ppermute x56, starting transfers between devices, between_chips(): moved[p] = lax.ppermute(x, 'wall', [(i, i ^ 2 * p) for i in range(n)])  82 us
    pallas_call x2, Pallas kernels, middle(): call(functools.partial(middle_kernel, chips), [whole_spec(c), whole_spec(...  23.7 us
    pallas_call x4, Pallas kernels, wall_operator(): call(functools.partial(wall_kernel, chips), [block(w_hi.shape)] * 2 + [bl...  22.3 us
    pallas_call x2, Pallas kernels, first(): call(first_kernel, [whole_spec(c), whole_spec(c), table_spec], [half_spec...  15.7 us
    pallas_call x2, Pallas kernels, last(): call(functools.partial(last_kernel, chips), [half_spec, half_spec, edge_s...  11.4 us
    ppermute x8, starting transfers between devices, between_cores(): return lax.ppermute(x, 'wall', [(i, i ^ 1) for i in range(n)])  11.3 us
  transfers between devices with their start and end apart: 68, of which 29 were waited for; matrix products, arithmetic and copies ran while one was open for 0% of the time, Pallas kernels for 15%

profile of v2, /device:TPU:11, one launch (start us, length us, event | category | flops | bytes accessed | tf_op | source)
XLA Modules:
  0.0 342.1 jit_solution(16407181862970028471)
XLA Ops:
  5.2 7.8 %first.2 = (f32[8,6,32,128]{3,2,1,0:T(8,128)S(1)}, f32[8,6,32,128]{3,2,1,0:T(8,128)S(1)}, f32[6,8,512]{2,1,0:T(8,128)S(1)}) custom-call(s32[2]{0:T(128)S(1)} %pad_add_fusion.me_ref, f32[8,2,12,32,128]{4,3,2,1,0:T(8,128)S(1)} %bitcast.10, s32[8,2,12,32,128]{4,3,2,1,0:T(8,128)S(1)} %bitcast.14, f32[8,128]{1,0:T(8,128)S(1)} %select_maximum_fusion.tab_ref), custom_call_target="tpu_custom_call" | custom-call | flops 39321600 | bytes 4718592 | tf_op jit(solution)/shard_map/first/pallas_call | solution.py:230
  15.8 7.9 %first.3 = (f32[8,6,32,128]{3,2,1,0:T(8,128)S(1)}, f32[8,6,32,128]{3,2,1,0:T(8,128)S(1)}, f32[6,8,512]{2,1,0:T(8,128)S(1)}) custom-call(s32[2]{0:T(128)S(1)} %pad_add_fusion.me_ref, f32[8,2,12,32,128]{4,3,2,1,0:T(8,128)S(1)} %bitcast.11, s32[8,2,12,32,128]{4,3,2,1,0:T(8,128)S(1)} %bitcast.15, f32[8,128]{1,0:T(8,128)S(1)} %select_maximum_fusion.tab_ref), custom_call_target="tpu_custom_call" | custom-call | flops 39321600 | bytes 4718592 | tf_op jit(solution)/shard_map/first/pallas_call | solution.py:230
  28.9 10.6 %collective-permute-done.7.refs_3_ = f32[2,6,32,128]{3,2,1,0:T(8,128)S(1)} collective-permute-done((f32[2,6,32,128]{3,2,1,0:T(8,128)S(1)}, f32[2,6,32,128]{3,2,1,0:T(8,128)S(1)}, u32[]{:S(2)}, u32[]{:S(2)}) %collective-permute-start.7) | collective-permute-done | bytes 196640 | tf_op jit(solution)/shard_map/ppermute | solution.py:285
  48.1 6.2 %collective-permute-done.8.refs_5_ = f32[2,6,32,128]{3,2,1,0:T(8,128)S(1)} collective-permute-done((f32[2,6,32,128]{3,2,1,0:T(8,128)S(1)}, f32[2,6,32,128]{3,2,1,0:T(8,128)S(1)}, u32[]{:S(2)}, u32[]{:S(2)}) %collective-permute-start.8) | collective-permute-done | bytes 196640 | tf_op jit(solution)/shard_map/ppermute | solution.py:285
  59.1 5.7 %collective-permute-done.11.refs_4_ = f32[2,6,32,128]{3,2,1,0:T(8,128)S(1)} collective-permute-done((f32[2,6,32,128]{3,2,1,0:T(8,128)S(1)}, f32[2,6,32,128]{3,2,1,0:T(8,128)S(1)}, u32[]{:S(2)}, u32[]{:S(2)}) %collective-permute-start.11) | collective-permute-done | bytes 196640 | tf_op jit(solution)/shard_map/ppermute | solution.py:285
  73.2 5.6 %wall.5 = (f32[2,6,32,128]{3,2,1,0:T(8,128)S(1)}, f32[2,6,32,128]{3,2,1,0:T(8,128)S(1)}, f32[2,6,32,128]{3,2,1,0:T(8,128)S(1)}, f32[2,6,32,128]{3,2,1,0:T(8,128)...) custom-call(s32[2]{0:T(128)S(1)} %pad_add_fusion.me_ref, ...), custom_call_target="tpu_custom_call" | custom-call | flops 2423783424 | bytes 4718592 | tf_op jit(solution)/shard_map/wall/pallas_call | solution.py:254
  78.8 7.1 %collective-permute-done.12.refs_6_ = f32[2,6,32,128]{3,2,1,0:T(8,128)S(1)} collective-permute-done((f32[2,6,32,128]{3,2,1,0:T(8,128)S(1)}, f32[2,6,32,128]{3,2,1,0:T(8,128)S(1)}, u32[]{:S(2)}, u32[]{:S(2)}) %collective-permute-start.12) | collective-permute-done | bytes 196640 | tf_op jit(solution)/shard_map/ppermute | solution.py:285
  90.2 8.0 %collective-permute-done.16.refs_4_ = f32[2,6,32,128]{3,2,1,0:T(8,128)S(1)} collective-permute-done((f32[2,6,32,128]{3,2,1,0:T(8,128)S(1)}, f32[2,6,32,128]{3,2,1,0:T(8,128)S(1)}, u32[]{:S(2)}, u32[]{:S(2)}) %collective-permute-start.16) | collective-permute-done | bytes 196640 | tf_op jit(solution)/shard_map/ppermute | solution.py:285
  102.8 12.9 %collective-permute-start.25 = (f32[2,6,32,128]{3,2,1,0:T(8,128)S(1)}, f32[2,6,32,128]{3,2,1,0:T(8,128)S(1)}, u32[]{:S(2)}, u32[]{:S(2)}) collective-permute-start(f32[2,6,32,128]{3,2,1,0:T(8,128)S(1)} %get-tuple-element.182), channel_id=1, source_target_pairs={{0,20},{2,22},{4,16},{6,18},{8,28},{10,30},{12,24},{14,26},{16,4},... | collective-permute-start | bytes 589832 | tf_op jit(solution)/shard_map/ppermute | solution.py:285
  139.4 6.5 %collective-permute-done.29.refs_4_ = f32[2,6,32,128]{3,2,1,0:T(8,128)S(1)} collective-permute-done((f32[2,6,32,128]{3,2,1,0:T(8,128)S(1)}, f32[2,6,32,128]{3,2,1,0:T(8,128)S(1)}, u32[]{:S(2)}, u32[]{:S(2)}) %collective-permute-start.29) | collective-permute-done | bytes 196640 | tf_op jit(solution)/shard_map/ppermute | solution.py:285
  146.3 6.9 %collective-permute-done.26.refs_7_ = f32[2,6,32,128]{3,2,1,0:T(8,128)S(1)} collective-permute-done((f32[2,6,32,128]{3,2,1,0:T(8,128)S(1)}, f32[2,6,32,128]{3,2,1,0:T(8,128)S(1)}, u32[]{:S(2)}, u32[]{:S(2)}) %collective-permute-start.26) | collective-permute-done | bytes 196640 | tf_op jit(solution)/shard_map/ppermute | solution.py:285
  165.4 11.9 %middle.3 = (f32[8,6,32,128]{3,2,1,0:T(8,128)S(1)}, f32[8,6,32,128]{3,2,1,0:T(8,128)S(1)}, f32[2,8,6,32,128]{4,3,2,1,0:T(8,128)S(1)}, f32[6,8,512]{2,1,0:T(8,128)S(1)}) custom-call(s32[2]{0:T(128)S(1)} %pad_add_fusion.me_ref, f32[8,2,12,32,128]{4,3,2,1,0:T(8,128)S(1)} %bitcast.12, s32[8,2,12,32,128]{4,3,2,1,0:T(8,128)S(1)} %bitcast.16, ...), custom_call_target="tpu_custom_call" | custom-call | flops 55050240 | bytes 9437184 | tf_op jit(solution)/shard_map/middle/pallas_call | solution.py:236
  177.5 11.8 %middle.2 = (f32[8,6,32,128]{3,2,1,0:T(8,128)S(1)}, f32[8,6,32,128]{3,2,1,0:T(8,128)S(1)}, f32[2,8,6,32,128]{4,3,2,1,0:T(8,128)S(1)}, f32[6,8,512]{2,1,0:T(8,128)S(1)}) custom-call(s32[2]{0:T(128)S(1)} %pad_add_fusion.me_ref, f32[8,2,12,32,128]{4,3,2,1,0:T(8,128)S(1)} %bitcast.13, s32[8,2,12,32,128]{4,3,2,1,0:T(8,128)S(1)} %bitcast.17, ...), custom_call_target="tpu_custom_call" | custom-call | flops 55050240 | bytes 9437184 | tf_op jit(solution)/shard_map/middle/pallas_call | solution.py:236
  200.5 6.4 %collective-permute-done.41.refs_3_ = f32[2,6,32,128]{3,2,1,0:T(8,128)S(1)} collective-permute-done((f32[2,6,32,128]{3,2,1,0:T(8,128)S(1)}, f32[2,6,32,128]{3,2,1,0:T(8,128)S(1)}, u32[]{:S(2)}, u32[]{:S(2)}) %collective-permute-start.41) | collective-permute-done | bytes 196640 | tf_op jit(solution)/shard_map/ppermute | solution.py:285
  210.7 6.8 %collective-permute-done.37.refs_6_ = f32[2,6,32,128]{3,2,1,0:T(8,128)S(1)} collective-permute-done((f32[2,6,32,128]{3,2,1,0:T(8,128)S(1)}, f32[2,6,32,128]{3,2,1,0:T(8,128)S(1)}, u32[]{:S(2)}, u32[]{:S(2)}) %collective-permute-start.37) | collective-permute-done | bytes 196640 | tf_op jit(solution)/shard_map/ppermute | solution.py:285
  222.8 11.5 %collective-permute-done.42.refs_5_ = f32[2,6,32,128]{3,2,1,0:T(8,128)S(1)} collective-permute-done((f32[2,6,32,128]{3,2,1,0:T(8,128)S(1)}, f32[2,6,32,128]{3,2,1,0:T(8,128)S(1)}, u32[]{:S(2)}, u32[]{:S(2)}) %collective-permute-start.42) | collective-permute-done | bytes 196640 | tf_op jit(solution)/shard_map/ppermute | solution.py:285
  244.4 7.0 %collective-permute-start.50 = (f32[2,6,32,128]{3,2,1,0:T(8,128)S(1)}, f32[2,6,32,128]{3,2,1,0:T(8,128)S(1)}, u32[]{:S(2)}, u32[]{:S(2)}) collective-permute-start(f32[2,6,32,128]{3,2,1,0:T(8,128)S(1)} %get-tuple-element.226), channel_id=1, source_target_pairs={{0,20},{2,22},{4,16},{6,18},{8,28},{10,30},{12,24},{14,26},{16,4},... | collective-permute-start | bytes 589832 | tf_op jit(solution)/shard_map/ppermute | solution.py:285
  254.4 7.4 %collective-permute-done.50.refs_4_ = f32[2,6,32,128]{3,2,1,0:T(8,128)S(1)} collective-permute-done((f32[2,6,32,128]{3,2,1,0:T(8,128)S(1)}, f32[2,6,32,128]{3,2,1,0:T(8,128)S(1)}, u32[]{:S(2)}, u32[]{:S(2)}) %collective-permute-start.50) | collective-permute-done | bytes 196640 | tf_op jit(solution)/shard_map/ppermute | solution.py:285
  261.8 6.5 %collective-permute-done.55.refs_4_ = f32[2,6,32,128]{3,2,1,0:T(8,128)S(1)} collective-permute-done((f32[2,6,32,128]{3,2,1,0:T(8,128)S(1)}, f32[2,6,32,128]{3,2,1,0:T(8,128)S(1)}, u32[]{:S(2)}, u32[]{:S(2)}) %collective-permute-start.55) | collective-permute-done | bytes 196640 | tf_op jit(solution)/shard_map/ppermute | solution.py:285
  276.4 5.6 %wall.6 = (f32[2,6,32,128]{3,2,1,0:T(8,128)S(1)}, f32[2,6,32,128]{3,2,1,0:T(8,128)S(1)}, f32[2,6,32,128]{3,2,1,0:T(8,128)S(1)}, f32[2,6,32,128]{3,2,1,0:T(8,128)...) custom-call(s32[2]{0:T(128)S(1)} %pad_add_fusion.me_ref, ...), custom_call_target="tpu_custom_call" | custom-call | flops 2423783424 | bytes 4718592 | tf_op jit(solution)/shard_map/wall/pallas_call | solution.py:254
  282.8 10.2 %collective-permute-done.52.refs_7_ = f32[2,6,32,128]{3,2,1,0:T(8,128)S(1)} collective-permute-done((f32[2,6,32,128]{3,2,1,0:T(8,128)S(1)}, f32[2,6,32,128]{3,2,1,0:T(8,128)S(1)}, u32[]{:S(2)}, u32[]{:S(2)}) %collective-permute-start.52) | collective-permute-done | bytes 196640 | tf_op jit(solution)/shard_map/ppermute | solution.py:285
  306.0 12.7 %collective-permute-done.60.refs_7_ = f32[2,6,32,128]{3,2,1,0:T(8,128)S(1)} collective-permute-done((f32[2,6,32,128]{3,2,1,0:T(8,128)S(1)}, f32[2,6,32,128]{3,2,1,0:T(8,128)S(1)}, u32[]{:S(2)}, u32[]{:S(2)}) %collective-permute-start.60) | collective-permute-done | bytes 196640 | tf_op jit(solution)/shard_map/ppermute | solution.py:285
  330.7 5.7 %last.2 = (f32[8,2,12,32,128]{4,3,2,1,0:T(8,128)}, f32[8,2,12,32,128]{4,3,2,1,0:T(8,128)}) custom-call(s32[2]{0:T(128)S(1)} %pad_add_fusion.me_ref, f32[8,6,32,128]{3,2,1,0:T(8,128)S(1)} %get-tuple-element.199.same_ref, f32[8,6,32,128]{3,2,1,0:T(8,128)S(1)} %get-tuple-element.200.other_ref, f32[6,8,512]{2,1,0:T(8,128)S(1)} %collective-permute-done.38.halo_ref, ...), custom_call_target="tpu_custom_call" | custom-call | flops 15728640 | bytes 7864320 | tf_op jit(solution)/shard_map/last/pallas_call | solution.py:243
  336.4 5.7 %last.3 = (f32[8,2,12,32,128]{4,3,2,1,0:T(8,128)}, f32[8,2,12,32,128]{4,3,2,1,0:T(8,128)}) custom-call(s32[2]{0:T(128)S(1)} %pad_add_fusion.me_ref, f32[8,6,32,128]{3,2,1,0:T(8,128)S(1)} %get-tuple-element.193.same_ref, f32[8,6,32,128]{3,2,1,0:T(8,128)S(1)} %get-tuple-element.194.other_ref, ...), custom_call_target="tpu_custom_call", output_to_operand_aliasing={{0}: (14, {}), {1}: (15, {})} | custom-call | flops 15728640 | bytes 7864320 | tf_op jit(solution)/shard_map/last/pallas_call | solution.py:243
  (143 shorter events, 146.9 us)
Async XLA Ops:
  23.7 24.3 %collective-permute-start.2 = (f32[8,6,32,128]{3,2,1,0:T(8,128)S(1)}, f32[8,6,32,128]{3,2,1,0:T(8,128)S(1)}, u32[]{:S(2)}, u32[]{:S(2)}) collective-permute-start(f32[8,6,32,128]{3,2,1,0:T(8,128)S(1)} %get-tuple-element.138.other_ref), channel_id=1, source_target_pairs={{0,2},{2,0},{4,6},{6,4},{8,10},{10,8},{12,14},{14,12},{16,18},{18,... | collective-permute-start | bytes 2359304 | tf_op jit(solution)/shard_map/ppermute | solution.py:291
  64.8 21.1 %collective-permute-start.12 = (f32[2,6,32,128]{3,2,1,0:T(8,128)S(1)}, f32[2,6,32,128]{3,2,1,0:T(8,128)S(1)}, u32[]{:S(2)}, u32[]{:S(2)}) collective-permute-start(f32[2,6,32,128]{3,2,1,0:T(8,128)S(1)} %get-tuple-element.155), channel_id=1, source_target_pairs={{0,28},{2,30},{4,24},{6,26},{8,20},{10,22},{12,16},{14,18},{16,12}... | collective-permute-start | bytes 589832 | tf_op jit(solution)/shard_map/ppermute | solution.py:285
  64.8 21.1 %collective-permute-start.6 = (f32[2,6,32,128]{3,2,1,0:T(8,128)S(1)}, f32[2,6,32,128]{3,2,1,0:T(8,128)S(1)}, u32[]{:S(2)}, u32[]{:S(2)}) collective-permute-start(f32[2,6,32,128]{3,2,1,0:T(8,128)S(1)} %get-tuple-element.145), channel_id=1, source_target_pairs={{0,4},{2,6},{4,0},{6,2},{8,12},{10,14},{12,8},{14,10},{16,20},{18,... | collective-permute-start | bytes 589832 | tf_op jit(solution)/shard_map/ppermute | solution.py:285
  69.0 21.2 %collective-permute-start.17 = (f32[2,6,32,128]{3,2,1,0:T(8,128)S(1)}, f32[2,6,32,128]{3,2,1,0:T(8,128)S(1)}, u32[]{:S(2)}, u32[]{:S(2)}) collective-permute-start(f32[2,6,32,128]{3,2,1,0:T(8,128)S(1)} %get-tuple-element.163), channel_id=1, source_target_pairs={{0,24},{2,26},{4,28},{6,30},{8,16},{10,18},{12,20},{14,22},{16,8},... | collective-permute-start | bytes 589832 | tf_op jit(solution)/shard_map/ppermute | solution.py:285
  69.0 29.2 %collective-permute-start.16 = (f32[2,6,32,128]{3,2,1,0:T(8,128)S(1)}, f32[2,6,32,128]{3,2,1,0:T(8,128)S(1)}, u32[]{:S(2)}, u32[]{:S(2)}) collective-permute-start(f32[2,6,32,128]{3,2,1,0:T(8,128)S(1)} %get-tuple-element.161), channel_id=1, source_target_pairs={{0,20},{2,22},{4,16},{6,18},{8,28},{10,30},{12,24},{14,26},{16,4},... | collective-permute-start | bytes 589832 | tf_op jit(solution)/shard_map/ppermute | solution.py:285
  98.2 21.3 %collective-permute-start.18 = (f32[2,6,32,128]{3,2,1,0:T(8,128)S(1)}, f32[2,6,32,128]{3,2,1,0:T(8,128)S(1)}, u32[]{:S(2)}, u32[]{:S(2)}) collective-permute-start(f32[2,6,32,128]{3,2,1,0:T(8,128)S(1)} %get-tuple-element.168), channel_id=1, source_target_pairs={{0,28},{2,30},{4,24},{6,26},{8,20},{10,22},{12,16},{14,18},{16,12}... | collective-permute-start | bytes 589832 | tf_op jit(solution)/shard_map/ppermute | solution.py:285
  98.2 28.5 %collective-permute-start.28 = (f32[2,6,32,128]{3,2,1,0:T(8,128)S(1)}, f32[2,6,32,128]{3,2,1,0:T(8,128)S(1)}, u32[]{:S(2)}, u32[]{:S(2)}) collective-permute-start(f32[2,6,32,128]{3,2,1,0:T(8,128)S(1)} %get-tuple-element.187), channel_id=1, source_target_pairs={{0,4},{2,6},{4,0},{6,2},{8,12},{10,14},{12,8},{14,10},{16,20},{18,... | collective-permute-start | bytes 589832 | tf_op jit(solution)/shard_map/ppermute | solution.py:285
  102.8 22.4 %collective-permute-start.22 = (f32[2,6,32,128]{3,2,1,0:T(8,128)S(1)}, f32[2,6,32,128]{3,2,1,0:T(8,128)S(1)}, u32[]{:S(2)}, u32[]{:S(2)}) collective-permute-start(f32[2,6,32,128]{3,2,1,0:T(8,128)S(1)} %get-tuple-element.175), channel_id=1, source_target_pairs={{0,24},{2,26},{4,28},{6,30},{8,16},{10,18},{12,20},{14,22},{16,8},... | collective-permute-start | bytes 589832 | tf_op jit(solution)/shard_map/ppermute | solution.py:285
  102.8 26.9 %collective-permute-start.25 = (f32[2,6,32,128]{3,2,1,0:T(8,128)S(1)}, f32[2,6,32,128]{3,2,1,0:T(8,128)S(1)}, u32[]{:S(2)}, u32[]{:S(2)}) collective-permute-start(f32[2,6,32,128]{3,2,1,0:T(8,128)S(1)} %get-tuple-element.182), channel_id=1, source_target_pairs={{0,20},{2,22},{4,16},{6,18},{8,28},{10,30},{12,24},{14,26},{16,4},... | collective-permute-start | bytes 589832 | tf_op jit(solution)/shard_map/ppermute | solution.py:285
  129.7 23.6 %collective-permute-start.26 = (f32[2,6,32,128]{3,2,1,0:T(8,128)S(1)}, f32[2,6,32,128]{3,2,1,0:T(8,128)S(1)}, u32[]{:S(2)}, u32[]{:S(2)}) collective-permute-start(f32[2,6,32,128]{3,2,1,0:T(8,128)S(1)} %get-tuple-element.183), channel_id=1, source_target_pairs={{0,28},{2,30},{4,24},{6,26},{8,20},{10,22},{12,16},{14,18},{16,12}... | collective-permute-start | bytes 589832 | tf_op jit(solution)/shard_map/ppermute | solution.py:285
  130.1 35.3 %collective-permute-start.35 = (f32[8,6,32,128]{3,2,1,0:T(8,128)S(1)}, f32[8,6,32,128]{3,2,1,0:T(8,128)S(1)}, u32[]{:S(2)}, u32[]{:S(2)}) collective-permute-start(f32[8,6,32,128]{3,2,1,0:T(8,128)S(1)} %gather.5), channel_id=1, source_target_pairs={{0,2},{2,0},{4,6},{6,4},{8,10},{10,8},{12,14},{14,12},{16,18},{18,... | collective-permute-start | bytes 2359304 | tf_op jit(solution)/shard_map/ppermute | solution.py:291
  134.2 24.4 %collective-permute-start.30 = (f32[2,6,32,128]{3,2,1,0:T(8,128)S(1)}, f32[2,6,32,128]{3,2,1,0:T(8,128)S(1)}, u32[]{:S(2)}, u32[]{:S(2)}) collective-permute-start(f32[2,6,32,128]{3,2,1,0:T(8,128)S(1)} %get-tuple-element.190), channel_id=1, source_target_pairs={{0,20},{2,22},{4,16},{6,18},{8,28},{10,30},{12,24},{14,26},{16,4},... | collective-permute-start | bytes 589832 | tf_op jit(solution)/shard_map/ppermute | solution.py:285
  189.3 28.3 %collective-permute-start.34 = (f32[8,6,32,128]{3,2,1,0:T(8,128)S(1)}, f32[8,6,32,128]{3,2,1,0:T(8,128)S(1)}, u32[]{:S(2)}, u32[]{:S(2)}) collective-permute-start(f32[8,6,32,128]{3,2,1,0:T(8,128)S(1)} %get-tuple-element.194.other_ref), channel_id=1, source_target_pairs={{0,2},{2,0},{4,6},{6,4},{8,10},{10,8},{12,14},{14,12},{16,18},{18,... | collective-permute-start | bytes 2359304 | tf_op jit(solution)/shard_map/ppermute | solution.py:291
  192.5 25.1 %collective-permute-start.37 = (f32[2,6,32,128]{3,2,1,0:T(8,128)S(1)}, f32[2,6,32,128]{3,2,1,0:T(8,128)S(1)}, u32[]{:S(2)}, u32[]{:S(2)}) collective-permute-start(f32[2,6,32,128]{3,2,1,0:T(8,128)S(1)} %get-tuple-element.203), channel_id=1, source_target_pairs={{0,28},{2,30},{4,24},{6,26},{8,20},{10,22},{12,16},{14,18},{16,12}... | collective-permute-start | bytes 589832 | tf_op jit(solution)/shard_map/ppermute | solution.py:285
  192.9 24.7 %collective-permute-start.48 = (f32[2,6,32,128]{3,2,1,0:T(8,128)S(1)}, f32[2,6,32,128]{3,2,1,0:T(8,128)S(1)}, u32[]{:S(2)}, u32[]{:S(2)}) collective-permute-start(f32[2,6,32,128]{3,2,1,0:T(8,128)S(1)} %get-tuple-element.223), channel_id=1, source_target_pairs={{0,4},{2,6},{4,0},{6,2},{8,12},{10,14},{12,8},{14,10},{16,20},{18,... | collective-permute-start | bytes 589832 | tf_op jit(solution)/shard_map/ppermute | solution.py:285
  210.7 23.6 %collective-permute-start.42 = (f32[2,6,32,128]{3,2,1,0:T(8,128)S(1)}, f32[2,6,32,128]{3,2,1,0:T(8,128)S(1)}, u32[]{:S(2)}, u32[]{:S(2)}) collective-permute-start(f32[2,6,32,128]{3,2,1,0:T(8,128)S(1)} %get-tuple-element.211), channel_id=1, source_target_pairs={{0,24},{2,26},{4,28},{6,30},{8,16},{10,18},{12,20},{14,22},{16,8},... | collective-permute-start | bytes 589832 | tf_op jit(solution)/shard_map/ppermute | solution.py:285
  222.0 22.4 %collective-permute-start.33 = (f32[6,8,512]{2,1,0:T(8,128)S(1)}, f32[6,8,512]{2,1,0:T(8,128)S(1)}, u32[]{:S(2)}, u32[]{:S(2)}) collective-permute-start(f32[6,8,512]{2,1,0:T(8,128)S(1)} %get-tuple-element.195), channel_id=1, source_target_pairs={{0,1},{1,0},{2,3},{3,2},{4,5},{5,4},{6,7},{7,6},{8,9},{9,8},{10,11... | collective-permute-start | bytes 294920 | tf_op jit(solution)/shard_map/ppermute | solution.py:296
  222.8 21.7 %collective-permute-start.46 = (f32[2,6,32,128]{3,2,1,0:T(8,128)S(1)}, f32[2,6,32,128]{3,2,1,0:T(8,128)S(1)}, u32[]{:S(2)}, u32[]{:S(2)}) collective-permute-start(f32[2,6,32,128]{3,2,1,0:T(8,128)S(1)} %get-tuple-element.219), channel_id=1, source_target_pairs={{0,28},{2,30},{4,24},{6,26},{8,20},{10,22},{12,16},{14,18},{16,12}... | collective-permute-start | bytes 589832 | tf_op jit(solution)/shard_map/ppermute | solution.py:285
  269.2 23.8 %collective-permute-start.52 = (f32[2,6,32,128]{3,2,1,0:T(8,128)S(1)}, f32[2,6,32,128]{3,2,1,0:T(8,128)S(1)}, u32[]{:S(2)}, u32[]{:S(2)}) collective-permute-start(f32[2,6,32,128]{3,2,1,0:T(8,128)S(1)} %get-tuple-element.233), channel_id=1, source_target_pairs={{0,28},{2,30},{4,24},{6,26},{8,20},{10,22},{12,16},{14,18},{16,12}... | collective-permute-start | bytes 589832 | tf_op jit(solution)/shard_map/ppermute | solution.py:285
  270.9 23.9 %collective-permute-start.59 = (f32[2,6,32,128]{3,2,1,0:T(8,128)S(1)}, f32[2,6,32,128]{3,2,1,0:T(8,128)S(1)}, u32[]{:S(2)}, u32[]{:S(2)}) collective-permute-start(f32[2,6,32,128]{3,2,1,0:T(8,128)S(1)} %get-tuple-element.247), channel_id=1, source_target_pairs={{0,20},{2,22},{4,16},{6,18},{8,28},{10,30},{12,24},{14,26},{16,4},... | collective-permute-start | bytes 589832 | tf_op jit(solution)/shard_map/ppermute | solution.py:285
  294.8 23.9 %collective-permute-start.60 = (f32[2,6,32,128]{3,2,1,0:T(8,128)S(1)}, f32[2,6,32,128]{3,2,1,0:T(8,128)S(1)}, u32[]{:S(2)}, u32[]{:S(2)}) collective-permute-start(f32[2,6,32,128]{3,2,1,0:T(8,128)S(1)} %get-tuple-element.248), channel_id=1, source_target_pairs={{0,28},{2,30},{4,24},{6,26},{8,20},{10,22},{12,16},{14,18},{16,12}... | collective-permute-start | bytes 589832 | tf_op jit(solution)/shard_map/ppermute | solution.py:285
  296.4 26.6 %collective-permute-start.64 = (f32[2,6,32,128]{3,2,1,0:T(8,128)S(1)}, f32[2,6,32,128]{3,2,1,0:T(8,128)S(1)}, u32[]{:S(2)}, u32[]{:S(2)}) collective-permute-start(f32[2,6,32,128]{3,2,1,0:T(8,128)S(1)} %get-tuple-element.255), channel_id=1, source_target_pairs={{0,20},{2,22},{4,16},{6,18},{8,28},{10,30},{12,24},{14,26},{16,4},... | collective-permute-start | bytes 589832 | tf_op jit(solution)/shard_map/ppermute | solution.py:285
  301.5 27.0 %collective-permute-start.65 = (f32[2,6,32,128]{3,2,1,0:T(8,128)S(1)}, f32[2,6,32,128]{3,2,1,0:T(8,128)S(1)}, u32[]{:S(2)}, u32[]{:S(2)}) collective-permute-start(f32[2,6,32,128]{3,2,1,0:T(8,128)S(1)} %get-tuple-element.257), channel_id=1, source_target_pairs={{0,24},{2,26},{4,28},{6,30},{8,16},{10,18},{12,20},{14,22},{16,8},... | collective-permute-start | bytes 589832 | tf_op jit(solution)/shard_map/ppermute | solution.py:285
  305.1 23.4 %collective-permute-start.54 = (f32[2,6,32,128]{3,2,1,0:T(8,128)S(1)}, f32[2,6,32,128]{3,2,1,0:T(8,128)S(1)}, u32[]{:S(2)}, u32[]{:S(2)}) collective-permute-start(f32[2,6,32,128]{3,2,1,0:T(8,128)S(1)} %get-tuple-element.235), channel_id=1, source_target_pairs={{0,4},{2,6},{4,0},{6,2},{8,12},{10,14},{12,8},{14,10},{16,20},{18,... | collective-permute-start | bytes 589832 | tf_op jit(solution)/shard_map/ppermute | solution.py:285
  (49 other events, 725.7 us)

commit v3 on v2

--- a/solution.py
+++ b/solution.py
@@ -18,9 +18,9 @@
 BF16 = jnp.bfloat16
 VMEM_BYTES = 24 * 1024 * 1024
 CHUNKS = (2, 3, 1)
-ORDER = (4, 2, 7, 1, 6, 5, 3)
+ORDER = (4, 7, 2, 6, 1, 5, 3)
 WINDOW = 4
-EARLY = 6
+EARLY = 4
 
 
 def inverse(x):
@@ -215,7 +215,7 @@
     cells = n * m * r * z
 
     def cost(ops, arrays, flops=0):
-        return pl.CostEstimate(flops=cells * ops + flops, bytes_accessed=cells * 4 * arrays, transcendentals=0)
+        return pl.CostEstimate(flops=1, bytes_accessed=1, transcendentals=0)
 
     def call(kernel, ins, outs, shapes, estimate, name, aliases={}, scratch=(), steps=m):
         grid = pltpu.PrefetchScalarGridSpec(

time: 345 us -> 341 us (0.988)
  waiting for transfers between devices: 165 us -> 155 us
  starting transfers between devices: 97.8 us -> 102 us
    ppermute x56, waiting for transfers between devices: 163 us -> 142 us  [between_chips(): moved[p] = lax.ppermute(x, 'wall', [(i, i ^ 2 * p) for i in range(n)])]
    ppermute x56, starting transfers between devices: 82 us -> 89.8 us  [between_chips(): moved[p] = lax.ppermute(x, 'wall', [(i, i ^ 2 * p) for i in range(n)])]
    ppermute x4, waiting for transfers between devices: 0.01 us -> 7.7 us  [neighbours(): return lax.ppermute(e, 'span', forward)]
    ppermute x8, starting transfers between devices: 11.3 us -> 6.83 us  [between_cores(): return lax.ppermute(x, 'wall', [(i, i ^ 1) for i in range(n)])]
    ppermute x8, waiting for transfers between devices: 1.93 us -> 5.67 us  [between_cores(): return lax.ppermute(x, 'wall', [(i, i ^ 1) for i in range(n)])]
  transfers between devices with their start and end apart: 68 -> 68, of which waited for: 29 -> 32; matrix products, arithmetic and copies ran while one was open for 0% -> 0% of each run, Pallas kernels for 15% -> 15%
where the time goes in v3:
time: 341 us; the launch traced here: 336 us
  waiting for transfers between devices  155 us (45%)
  starting transfers between devices  102 us (30%)
  Pallas kernels  73.6 us (22%)
  local copies, waits for them, and re-layouts  3.79 us (1%)
    ppermute x56, waiting for transfers between devices, between_chips(): moved[p] = lax.ppermute(x, 'wall', [(i, i ^ 2 * p) for i in range(n)])  142 us
    ppermute x56, starting transfers between devices, between_chips(): moved[p] = lax.ppermute(x, 'wall', [(i, i ^ 2 * p) for i in range(n)])  89.8 us
    pallas_call x2, Pallas kernels, middle(): call(functools.partial(middle_kernel, chips), [whole_spec(c), whole_spec(...  23.7 us
    pallas_call x4, Pallas kernels, wall_operator(): call(functools.partial(wall_kernel, chips), [block(w_hi.shape)] * 2 + [bl...  22.2 us
    pallas_call x2, Pallas kernels, first(): call(first_kernel, [whole_spec(c), whole_spec(c), table_spec], [half_spec...  15.7 us
    pallas_call x2, Pallas kernels, last(): call(functools.partial(last_kernel, chips), [half_spec, half_spec, edge_s...  11.4 us
    ppermute x4, waiting for transfers between devices, neighbours(): return lax.ppermute(e, 'span', forward)  7.7 us
    ppermute x8, starting transfers between devices, between_cores(): return lax.ppermute(x, 'wall', [(i, i ^ 1) for i in range(n)])  6.83 us
  transfers between devices with their start and end apart: 68, of which 32 were waited for; matrix products, arithmetic and copies ran while one was open for 0% of the time, Pallas kernels for 15%

profile of v3, /device:TPU:11, one launch (start us, length us, event | category | flops | bytes accessed | tf_op | source)
XLA Modules:
  0.0 335.9 jit_solution(15635606415481600340)
XLA Ops:
  5.2 7.8 %first.2 = (f32[8,6,32,128]{3,2,1,0:T(8,128)S(1)}, f32[8,6,32,128]{3,2,1,0:T(8,128)S(1)}, f32[6,8,512]{2,1,0:T(8,128)S(1)}) custom-call(s32[2]{0:T(128)S(1)} %pad_add_fusion.me_ref, f32[8,2,12,32,128]{4,3,2,1,0:T(8,128)S(1)} %bitcast.10, s32[8,2,12,32,128]{4,3,2,1,0:T(8,128)S(1)} %bitcast.14, f32[8,128]{1,0:T(8,128)S(1)} %select_maximum_fusion.tab_ref), custom_call_target="tpu_custom_call" | custom-call | flops 1 | bytes 1 | tf_op jit(solution)/shard_map/first/pallas_call | solution.py:230
  15.8 7.9 %first.3 = (f32[8,6,32,128]{3,2,1,0:T(8,128)S(1)}, f32[8,6,32,128]{3,2,1,0:T(8,128)S(1)}, f32[6,8,512]{2,1,0:T(8,128)S(1)}) custom-call(s32[2]{0:T(128)S(1)} %pad_add_fusion.me_ref, f32[8,2,12,32,128]{4,3,2,1,0:T(8,128)S(1)} %bitcast.11, s32[8,2,12,32,128]{4,3,2,1,0:T(8,128)S(1)} %bitcast.15, f32[8,128]{1,0:T(8,128)S(1)} %select_maximum_fusion.tab_ref), custom_call_target="tpu_custom_call" | custom-call | flops 1 | bytes 1 | tf_op jit(solution)/shard_map/first/pallas_call | solution.py:230
  28.0 7.3 %collective-permute-done.5.refs_3_ = f32[2,6,32,128]{3,2,1,0:T(8,128)S(1)} collective-permute-done((f32[2,6,32,128]{3,2,1,0:T(8,128)S(1)}, f32[2,6,32,128]{3,2,1,0:T(8,128)S(1)}, u32[]{:S(2)}, u32[]{:S(2)}) %collective-permute-start.5) | collective-permute-done | bytes 196640 | tf_op jit(solution)/shard_map/ppermute | solution.py:285
  41.2 8.5 %collective-permute-done.10.refs_6_ = f32[2,6,32,128]{3,2,1,0:T(8,128)S(1)} collective-permute-done((f32[2,6,32,128]{3,2,1,0:T(8,128)S(1)}, f32[2,6,32,128]{3,2,1,0:T(8,128)S(1)}, u32[]{:S(2)}, u32[]{:S(2)}) %collective-permute-start.10) | collective-permute-done | bytes 196640 | tf_op jit(solution)/shard_map/ppermute | solution.py:285
  56.7 14.1 %collective-permute-done.11.refs_4_ = f32[2,6,32,128]{3,2,1,0:T(8,128)S(1)} collective-permute-done((f32[2,6,32,128]{3,2,1,0:T(8,128)S(1)}, f32[2,6,32,128]{3,2,1,0:T(8,128)S(1)}, u32[]{:S(2)}, u32[]{:S(2)}) %collective-permute-start.11) | collective-permute-done | bytes 196640 | tf_op jit(solution)/shard_map/ppermute | solution.py:285
  72.2 5.5 %wall.4 = (f32[2,6,32,128]{3,2,1,0:T(8,128)S(1)}, f32[2,6,32,128]{3,2,1,0:T(8,128)S(1)}, f32[2,6,32,128]{3,2,1,0:T(8,128)S(1)}, f32[2,6,32,128]{3,2,1,0:T(8,128)...) custom-call(s32[2]{0:T(128)S(1)} %pad_add_fusion.me_ref, ...), custom_call_target="tpu_custom_call" | custom-call | flops 1 | bytes 1 | tf_op jit(solution)/shard_map/wall/pallas_call | solution.py:254
  87.0 6.4 %collective-permute-done.17.refs_5_ = f32[2,6,32,128]{3,2,1,0:T(8,128)S(1)} collective-permute-done((f32[2,6,32,128]{3,2,1,0:T(8,128)S(1)}, f32[2,6,32,128]{3,2,1,0:T(8,128)S(1)}, u32[]{:S(2)}, u32[]{:S(2)}) %collective-permute-start.17) | collective-permute-done | bytes 196640 | tf_op jit(solution)/shard_map/ppermute | solution.py:285
  93.4 7.1 %collective-permute-done.16.refs_4_ = f32[2,6,32,128]{3,2,1,0:T(8,128)S(1)} collective-permute-done((f32[2,6,32,128]{3,2,1,0:T(8,128)S(1)}, f32[2,6,32,128]{3,2,1,0:T(8,128)S(1)}, u32[]{:S(2)}, u32[]{:S(2)}) %collective-permute-start.16) | collective-permute-done | bytes 196640 | tf_op jit(solution)/shard_map/ppermute | solution.py:285
  105.4 5.5 %wall.5 = (f32[2,6,32,128]{3,2,1,0:T(8,128)S(1)}, f32[2,6,32,128]{3,2,1,0:T(8,128)S(1)}, f32[2,6,32,128]{3,2,1,0:T(8,128)S(1)}, f32[2,6,32,128]{3,2,1,0:T(8,128)...) custom-call(s32[2]{0:T(128)S(1)} %pad_add_fusion.me_ref, ...), custom_call_target="tpu_custom_call" | custom-call | flops 1 | bytes 1 | tf_op jit(solution)/shard_map/wall/pallas_call | solution.py:254
  112.2 8.6 %collective-permute-start.23 = (f32[2,6,32,128]{3,2,1,0:T(8,128)S(1)}, f32[2,6,32,128]{3,2,1,0:T(8,128)S(1)}, u32[]{:S(2)}, u32[]{:S(2)}) collective-permute-start(f32[2,6,32,128]{3,2,1,0:T(8,128)S(1)} %get-tuple-element.178), channel_id=1, source_target_pairs={{0,12},{2,14},{4,8},{6,10},{8,4},{10,6},{12,0},{14,2},{16,28},{18,... | collective-permute-start | bytes 589832 | tf_op jit(solution)/shard_map/ppermute | solution.py:285
  122.2 5.6 %collective-permute-done.23.refs_3_ = f32[2,6,32,128]{3,2,1,0:T(8,128)S(1)} collective-permute-done((f32[2,6,32,128]{3,2,1,0:T(8,128)S(1)}, f32[2,6,32,128]{3,2,1,0:T(8,128)S(1)}, u32[]{:S(2)}, u32[]{:S(2)}) %collective-permute-start.23) | collective-permute-done | bytes 196640 | tf_op jit(solution)/shard_map/ppermute | solution.py:285
  136.8 7.2 %collective-permute-done.30.refs_7_ = f32[2,6,32,128]{3,2,1,0:T(8,128)S(1)} collective-permute-done((f32[2,6,32,128]{3,2,1,0:T(8,128)S(1)}, f32[2,6,32,128]{3,2,1,0:T(8,128)S(1)}, u32[]{:S(2)}, u32[]{:S(2)}) %collective-permute-start.30) | collective-permute-done | bytes 196640 | tf_op jit(solution)/shard_map/ppermute | solution.py:285
  151.2 11.7 %middle.2 = (f32[8,6,32,128]{3,2,1,0:T(8,128)S(1)}, f32[8,6,32,128]{3,2,1,0:T(8,128)S(1)}, f32[2,8,6,32,128]{4,3,2,1,0:T(8,128)S(1)}, f32[6,8,512]{2,1,0:T(8,128)S(1)}) custom-call(s32[2]{0:T(128)S(1)} %pad_add_fusion.me_ref, f32[8,2,12,32,128]{4,3,2,1,0:T(8,128)S(1)} %bitcast.12, s32[8,2,12,32,128]{4,3,2,1,0:T(8,128)S(1)} %bitcast.16, ...), custom_call_target="tpu_custom_call" | custom-call | flops 1 | bytes 1 | tf_op jit(solution)/shard_map/middle/pallas_call | solution.py:236
  172.4 12.0 %middle.3 = (f32[8,6,32,128]{3,2,1,0:T(8,128)S(1)}, f32[8,6,32,128]{3,2,1,0:T(8,128)S(1)}, f32[2,8,6,32,128]{4,3,2,1,0:T(8,128)S(1)}, f32[6,8,512]{2,1,0:T(8,128)S(1)}) custom-call(s32[2]{0:T(128)S(1)} %pad_add_fusion.me_ref, f32[8,2,12,32,128]{4,3,2,1,0:T(8,128)S(1)} %bitcast.13, s32[8,2,12,32,128]{4,3,2,1,0:T(8,128)S(1)} %bitcast.17, ...), custom_call_target="tpu_custom_call" | custom-call | flops 1 | bytes 1 | tf_op jit(solution)/shard_map/middle/pallas_call | solution.py:236
  189.2 10.7 %collective-permute-done.39.refs_3_ = f32[2,6,32,128]{3,2,1,0:T(8,128)S(1)} collective-permute-done((f32[2,6,32,128]{3,2,1,0:T(8,128)S(1)}, f32[2,6,32,128]{3,2,1,0:T(8,128)S(1)}, u32[]{:S(2)}, u32[]{:S(2)}) %collective-permute-start.39) | collective-permute-done | bytes 196640 | tf_op jit(solution)/shard_map/ppermute | solution.py:285
  215.0 7.9 %collective-permute-done.45.refs_4_ = f32[2,6,32,128]{3,2,1,0:T(8,128)S(1)} collective-permute-done((f32[2,6,32,128]{3,2,1,0:T(8,128)S(1)}, f32[2,6,32,128]{3,2,1,0:T(8,128)S(1)}, u32[]{:S(2)}, u32[]{:S(2)}) %collective-permute-start.45) | collective-permute-done | bytes 196640 | tf_op jit(solution)/shard_map/ppermute | solution.py:285
  222.9 9.3 %collective-permute-start.47 = (f32[2,6,32,128]{3,2,1,0:T(8,128)S(1)}, f32[2,6,32,128]{3,2,1,0:T(8,128)S(1)}, u32[]{:S(2)}, u32[]{:S(2)}) collective-permute-start(f32[2,6,32,128]{3,2,1,0:T(8,128)S(1)} %get-tuple-element.221), channel_id=1, source_target_pairs={{0,8},{2,10},{4,12},{6,14},{8,0},{10,2},{12,4},{14,6},{16,24},{18,... | collective-permute-start | bytes 589832 | tf_op jit(solution)/shard_map/ppermute | solution.py:285
  232.3 5.5 %wall.6 = (f32[2,6,32,128]{3,2,1,0:T(8,128)S(1)}, f32[2,6,32,128]{3,2,1,0:T(8,128)S(1)}, f32[2,6,32,128]{3,2,1,0:T(8,128)S(1)}, f32[2,6,32,128]{3,2,1,0:T(8,128)...) custom-call(s32[2]{0:T(128)S(1)} %pad_add_fusion.me_ref, ...), custom_call_target="tpu_custom_call" | custom-call | flops 1 | bytes 1 | tf_op jit(solution)/shard_map/wall/pallas_call | solution.py:254
  246.1 6.4 %collective-permute-done.51.refs_5_ = f32[2,6,32,128]{3,2,1,0:T(8,128)S(1)} collective-permute-done((f32[2,6,32,128]{3,2,1,0:T(8,128)S(1)}, f32[2,6,32,128]{3,2,1,0:T(8,128)S(1)}, u32[]{:S(2)}, u32[]{:S(2)}) %collective-permute-start.51) | collective-permute-done | bytes 196640 | tf_op jit(solution)/shard_map/ppermute | solution.py:285
  271.0 5.6 %collective-permute-done.56.refs_2_ = f32[2,6,32,128]{3,2,1,0:T(8,128)S(1)} collective-permute-done((f32[2,6,32,128]{3,2,1,0:T(8,128)S(1)}, f32[2,6,32,128]{3,2,1,0:T(8,128)S(1)}, u32[]{:S(2)}, u32[]{:S(2)}) %collective-permute-start.56) | collective-permute-done | bytes 196640 | tf_op jit(solution)/shard_map/ppermute | solution.py:285
  295.9 6.1 %collective-permute-done.64.refs_7_ = f32[2,6,32,128]{3,2,1,0:T(8,128)S(1)} collective-permute-done((f32[2,6,32,128]{3,2,1,0:T(8,128)S(1)}, f32[2,6,32,128]{3,2,1,0:T(8,128)S(1)}, u32[]{:S(2)}, u32[]{:S(2)}) %collective-permute-start.64) | collective-permute-done | bytes 196640 | tf_op jit(solution)/shard_map/ppermute | solution.py:285
  310.5 5.7 %last.2 = (f32[8,2,12,32,128]{4,3,2,1,0:T(8,128)}, f32[8,2,12,32,128]{4,3,2,1,0:T(8,128)}) custom-call(s32[2]{0:T(128)S(1)} %pad_add_fusion.me_ref, f32[8,6,32,128]{3,2,1,0:T(8,128)S(1)} %get-tuple-element.183.same_ref, f32[8,6,32,128]{3,2,1,0:T(8,128)S(1)} %get-tuple-element.201.other_ref, f32[6,8,512]{2,1,0:T(8,128)S(1)} %collective-permute-done.42.halo_ref, ...), custom_call_target="tpu_custom_call" | custom-call | flops 1 | bytes 1 | tf_op jit(solution)/shard_map/last/pallas_call | solution.py:243
  321.5 5.7 %collective-permute-done.66.refs_6_ = f32[2,6,32,128]{3,2,1,0:T(8,128)S(1)} collective-permute-done((f32[2,6,32,128]{3,2,1,0:T(8,128)S(1)}, f32[2,6,32,128]{3,2,1,0:T(8,128)S(1)}, u32[]{:S(2)}, u32[]{:S(2)}) %collective-permute-start.66) | collective-permute-done | bytes 196640 | tf_op jit(solution)/shard_map/ppermute | solution.py:285
  330.2 5.7 %last.3 = (f32[8,2,12,32,128]{4,3,2,1,0:T(8,128)}, f32[8,2,12,32,128]{4,3,2,1,0:T(8,128)}) custom-call(s32[2]{0:T(128)S(1)} %pad_add_fusion.me_ref, f32[8,6,32,128]{3,2,1,0:T(8,128)S(1)} %get-tuple-element.195.same_ref, f32[8,6,32,128]{3,2,1,0:T(8,128)S(1)} %get-tuple-element.196.other_ref, ...), custom_call_target="tpu_custom_call", output_to_operand_aliasing={{0}: (14, {}), {1}: (15, {})} | custom-call | flops 1 | bytes 1 | tf_op jit(solution)/shard_map/last/pallas_call | solution.py:243
  (143 shorter events, 151.0 us)
Async XLA Ops:
  23.7 26.1 %collective-permute-start.2 = (f32[8,6,32,128]{3,2,1,0:T(8,128)S(1)}, f32[8,6,32,128]{3,2,1,0:T(8,128)S(1)}, u32[]{:S(2)}, u32[]{:S(2)}) collective-permute-start(f32[8,6,32,128]{3,2,1,0:T(8,128)S(1)} %get-tuple-element.138.other_ref), channel_id=1, source_target_pairs={{0,2},{2,0},{4,6},{6,4},{8,10},{10,8},{12,14},{14,12},{16,18},{18,... | collective-permute-start | bytes 2359304 | tf_op jit(solution)/shard_map/ppermute | solution.py:291
  27.9 21.9 %collective-permute-start.10 = (f32[2,6,32,128]{3,2,1,0:T(8,128)S(1)}, f32[2,6,32,128]{3,2,1,0:T(8,128)S(1)}, u32[]{:S(2)}, u32[]{:S(2)}) collective-permute-start(f32[2,6,32,128]{3,2,1,0:T(8,128)S(1)} %get-tuple-element.151), channel_id=1, source_target_pairs={{0,28},{2,30},{4,24},{6,26},{8,20},{10,22},{12,16},{14,18},{16,12}... | collective-permute-start | bytes 589832 | tf_op jit(solution)/shard_map/ppermute | solution.py:285
  35.8 36.4 %collective-permute-start.9 = (f32[2,6,32,128]{3,2,1,0:T(8,128)S(1)}, f32[2,6,32,128]{3,2,1,0:T(8,128)S(1)}, u32[]{:S(2)}, u32[]{:S(2)}) collective-permute-start(f32[2,6,32,128]{3,2,1,0:T(8,128)S(1)} %get-tuple-element.149), channel_id=1, source_target_pairs={{0,12},{2,14},{4,8},{6,10},{8,4},{10,6},{12,0},{14,2},{16,28},{18,... | collective-permute-start | bytes 589832 | tf_op jit(solution)/shard_map/ppermute | solution.py:285
  49.8 21.1 %collective-permute-start.11 = (f32[2,6,32,128]{3,2,1,0:T(8,128)S(1)}, f32[2,6,32,128]{3,2,1,0:T(8,128)S(1)}, u32[]{:S(2)}, u32[]{:S(2)}) collective-permute-start(f32[2,6,32,128]{3,2,1,0:T(8,128)S(1)} %get-tuple-element.152), channel_id=1, source_target_pairs={{0,20},{2,22},{4,16},{6,18},{8,28},{10,30},{12,24},{14,26},{16,4},... | collective-permute-start | bytes 589832 | tf_op jit(solution)/shard_map/ppermute | solution.py:285
  54.0 25.8 %collective-permute-start.15 = (f32[2,6,32,128]{3,2,1,0:T(8,128)S(1)}, f32[2,6,32,128]{3,2,1,0:T(8,128)S(1)}, u32[]{:S(2)}, u32[]{:S(2)}) collective-permute-start(f32[2,6,32,128]{3,2,1,0:T(8,128)S(1)} %get-tuple-element.161), channel_id=1, source_target_pairs={{0,28},{2,30},{4,24},{6,26},{8,20},{10,22},{12,16},{14,18},{16,12}... | collective-permute-start | bytes 589832 | tf_op jit(solution)/shard_map/ppermute | solution.py:285
  56.2 24.4 %collective-permute-start.4 = (f32[2,6,32,128]{3,2,1,0:T(8,128)S(1)}, f32[2,6,32,128]{3,2,1,0:T(8,128)S(1)}, u32[]{:S(2)}, u32[]{:S(2)}) collective-permute-start(f32[2,6,32,128]{3,2,1,0:T(8,128)S(1)} %get-tuple-element.143), channel_id=1, source_target_pairs={{0,16},{2,18},{4,20},{6,22},{8,24},{10,26},{12,28},{14,30},{16,0},... | collective-permute-start | bytes 589832 | tf_op jit(solution)/shard_map/ppermute | solution.py:285
  79.8 20.7 %collective-permute-start.16 = (f32[2,6,32,128]{3,2,1,0:T(8,128)S(1)}, f32[2,6,32,128]{3,2,1,0:T(8,128)S(1)}, u32[]{:S(2)}, u32[]{:S(2)}) collective-permute-start(f32[2,6,32,128]{3,2,1,0:T(8,128)S(1)} %get-tuple-element.162), channel_id=1, source_target_pairs={{0,20},{2,22},{4,16},{6,18},{8,28},{10,30},{12,24},{14,26},{16,4},... | collective-permute-start | bytes 589832 | tf_op jit(solution)/shard_map/ppermute | solution.py:285
  80.6 23.3 %collective-permute-start.12 = (f32[2,6,32,128]{3,2,1,0:T(8,128)S(1)}, f32[2,6,32,128]{3,2,1,0:T(8,128)S(1)}, u32[]{:S(2)}, u32[]{:S(2)}) collective-permute-start(f32[2,6,32,128]{3,2,1,0:T(8,128)S(1)} %get-tuple-element.154), channel_id=1, source_target_pairs={{0,4},{2,6},{4,0},{6,2},{8,12},{10,14},{12,8},{14,10},{16,20},{18,... | collective-permute-start | bytes 589832 | tf_op jit(solution)/shard_map/ppermute | solution.py:285
  85.0 20.0 %collective-permute-start.14 = (f32[2,6,32,128]{3,2,1,0:T(8,128)S(1)}, f32[2,6,32,128]{3,2,1,0:T(8,128)S(1)}, u32[]{:S(2)}, u32[]{:S(2)}) collective-permute-start(f32[2,6,32,128]{3,2,1,0:T(8,128)S(1)} %get-tuple-element.158), channel_id=1, source_target_pairs={{0,12},{2,14},{4,8},{6,10},{8,4},{10,6},{12,0},{14,2},{16,28},{18,... | collective-permute-start | bytes 589832 | tf_op jit(solution)/shard_map/ppermute | solution.py:285
  131.2 20.0 %collective-permute-start.26 = (f32[8,6,32,128]{3,2,1,0:T(8,128)S(1)}, f32[8,6,32,128]{3,2,1,0:T(8,128)S(1)}, u32[]{:S(2)}, u32[]{:S(2)}) collective-permute-start(f32[8,6,32,128]{3,2,1,0:T(8,128)S(1)} %gather.4), channel_id=1, source_target_pairs={{0,2},{2,0},{4,6},{6,4},{8,10},{10,8},{12,14},{14,12},{16,18},{18,... | collective-permute-start | bytes 2359304 | tf_op jit(solution)/shard_map/ppermute | solution.py:291
  136.8 26.1 %collective-permute-start.19 = (f32[2,6,32,128]{3,2,1,0:T(8,128)S(1)}, f32[2,6,32,128]{3,2,1,0:T(8,128)S(1)}, u32[]{:S(2)}, u32[]{:S(2)}) collective-permute-start(f32[2,6,32,128]{3,2,1,0:T(8,128)S(1)} %get-tuple-element.170), channel_id=1, source_target_pairs={{0,16},{2,18},{4,20},{6,22},{8,24},{10,26},{12,28},{14,30},{16,0},... | collective-permute-start | bytes 589832 | tf_op jit(solution)/shard_map/ppermute | solution.py:285
  144.0 19.6 %collective-permute-start.31 = (f32[2,6,32,128]{3,2,1,0:T(8,128)S(1)}, f32[2,6,32,128]{3,2,1,0:T(8,128)S(1)}, u32[]{:S(2)}, u32[]{:S(2)}) collective-permute-start(f32[2,6,32,128]{3,2,1,0:T(8,128)S(1)} %get-tuple-element.192), channel_id=1, source_target_pairs={{0,20},{2,22},{4,16},{6,18},{8,28},{10,30},{12,24},{14,26},{16,4},... | collective-permute-start | bytes 589832 | tf_op jit(solution)/shard_map/ppermute | solution.py:285
  144.9 23.8 %collective-permute-start.32 = (f32[2,6,32,128]{3,2,1,0:T(8,128)S(1)}, f32[2,6,32,128]{3,2,1,0:T(8,128)S(1)}, u32[]{:S(2)}, u32[]{:S(2)}) collective-permute-start(f32[2,6,32,128]{3,2,1,0:T(8,128)S(1)} %get-tuple-element.194), channel_id=1, source_target_pairs={{0,24},{2,26},{4,28},{6,30},{8,16},{10,18},{12,20},{14,22},{16,8},... | collective-permute-start | bytes 589832 | tf_op jit(solution)/shard_map/ppermute | solution.py:285
  148.4 20.2 %collective-permute-start.29 = (f32[2,6,32,128]{3,2,1,0:T(8,128)S(1)}, f32[2,6,32,128]{3,2,1,0:T(8,128)S(1)}, u32[]{:S(2)}, u32[]{:S(2)}) collective-permute-start(f32[2,6,32,128]{3,2,1,0:T(8,128)S(1)} %get-tuple-element.188), channel_id=1, source_target_pairs={{0,12},{2,14},{4,8},{6,10},{8,4},{10,6},{12,0},{14,2},{16,28},{18,... | collective-permute-start | bytes 589832 | tf_op jit(solution)/shard_map/ppermute | solution.py:285
  184.4 28.4 %collective-permute-start.35 = (f32[8,6,32,128]{3,2,1,0:T(8,128)S(1)}, f32[8,6,32,128]{3,2,1,0:T(8,128)S(1)}, u32[]{:S(2)}, u32[]{:S(2)}) collective-permute-start(f32[8,6,32,128]{3,2,1,0:T(8,128)S(1)} %get-tuple-element.196.other_ref), channel_id=1, source_target_pairs={{0,2},{2,0},{4,6},{6,4},{8,10},{10,8},{12,14},{14,12},{16,18},{18,... | collective-permute-start | bytes 2359304 | tf_op jit(solution)/shard_map/ppermute | solution.py:291
  189.2 20.4 %collective-permute-start.41 = (f32[2,6,32,128]{3,2,1,0:T(8,128)S(1)}, f32[2,6,32,128]{3,2,1,0:T(8,128)S(1)}, u32[]{:S(2)}, u32[]{:S(2)}) collective-permute-start(f32[2,6,32,128]{3,2,1,0:T(8,128)S(1)} %get-tuple-element.210), channel_id=1, source_target_pairs={{0,8},{2,10},{4,12},{6,14},{8,0},{10,2},{12,4},{14,6},{16,24},{18,... | collective-permute-start | bytes 589832 | tf_op jit(solution)/shard_map/ppermute | solution.py:285
  209.6 22.7 %collective-permute-start.43 = (f32[2,6,32,128]{3,2,1,0:T(8,128)S(1)}, f32[2,6,32,128]{3,2,1,0:T(8,128)S(1)}, u32[]{:S(2)}, u32[]{:S(2)}) collective-permute-start(f32[2,6,32,128]{3,2,1,0:T(8,128)S(1)} %get-tuple-element.213), channel_id=1, source_target_pairs={{0,12},{2,14},{4,8},{6,10},{8,4},{10,6},{12,0},{14,2},{16,28},{18,... | collective-permute-start | bytes 589832 | tf_op jit(solution)/shard_map/ppermute | solution.py:285
  212.9 26.1 %collective-permute-start.49 = (f32[2,6,32,128]{3,2,1,0:T(8,128)S(1)}, f32[2,6,32,128]{3,2,1,0:T(8,128)S(1)}, u32[]{:S(2)}, u32[]{:S(2)}) collective-permute-start(f32[2,6,32,128]{3,2,1,0:T(8,128)S(1)} %get-tuple-element.226), channel_id=1, source_target_pairs={{0,28},{2,30},{4,24},{6,26},{8,20},{10,22},{12,16},{14,18},{16,12}... | collective-permute-start | bytes 589832 | tf_op jit(solution)/shard_map/ppermute | solution.py:285
  213.9 26.7 %collective-permute-start.38 = (f32[2,6,32,128]{3,2,1,0:T(8,128)S(1)}, f32[2,6,32,128]{3,2,1,0:T(8,128)S(1)}, u32[]{:S(2)}, u32[]{:S(2)}) collective-permute-start(f32[2,6,32,128]{3,2,1,0:T(8,128)S(1)} %get-tuple-element.204), channel_id=1, source_target_pairs={{0,16},{2,18},{4,20},{6,22},{8,24},{10,26},{12,28},{14,30},{16,0},... | collective-permute-start | bytes 589832 | tf_op jit(solution)/shard_map/ppermute | solution.py:285
  222.9 22.0 %collective-permute-start.47 = (f32[2,6,32,128]{3,2,1,0:T(8,128)S(1)}, f32[2,6,32,128]{3,2,1,0:T(8,128)S(1)}, u32[]{:S(2)}, u32[]{:S(2)}) collective-permute-start(f32[2,6,32,128]{3,2,1,0:T(8,128)S(1)} %get-tuple-element.221), channel_id=1, source_target_pairs={{0,8},{2,10},{4,12},{6,14},{8,0},{10,2},{12,4},{14,6},{16,24},{18,... | collective-permute-start | bytes 589832 | tf_op jit(solution)/shard_map/ppermute | solution.py:285
  240.6 22.1 %collective-permute-start.46 = (f32[2,6,32,128]{3,2,1,0:T(8,128)S(1)}, f32[2,6,32,128]{3,2,1,0:T(8,128)S(1)}, u32[]{:S(2)}, u32[]{:S(2)}) collective-permute-start(f32[2,6,32,128]{3,2,1,0:T(8,128)S(1)} %get-tuple-element.219), channel_id=1, source_target_pairs={{0,4},{2,6},{4,0},{6,2},{8,12},{10,14},{12,8},{14,10},{16,20},{18,... | collective-permute-start | bytes 589832 | tf_op jit(solution)/shard_map/ppermute | solution.py:285
  289.3 21.2 %collective-permute-start.60 = (f32[8,6,32,128]{3,2,1,0:T(8,128)S(1)}, f32[8,6,32,128]{3,2,1,0:T(8,128)S(1)}, u32[]{:S(2)}, u32[]{:S(2)}) collective-permute-start(f32[8,6,32,128]{3,2,1,0:T(8,128)S(1)} %gather.6), channel_id=1, source_target_pairs={{0,2},{2,0},{4,6},{6,4},{8,10},{10,8},{12,14},{14,12},{16,18},{18,... | collective-permute-start | bytes 2359304 | tf_op jit(solution)/shard_map/ppermute | solution.py:291
  295.8 20.4 %collective-permute-start.53 = (f32[2,6,32,128]{3,2,1,0:T(8,128)S(1)}, f32[2,6,32,128]{3,2,1,0:T(8,128)S(1)}, u32[]{:S(2)}, u32[]{:S(2)}) collective-permute-start(f32[2,6,32,128]{3,2,1,0:T(8,128)S(1)} %get-tuple-element.235), channel_id=1, source_target_pairs={{0,16},{2,18},{4,20},{6,22},{8,24},{10,26},{12,28},{14,30},{16,0},... | collective-permute-start | bytes 589832 | tf_op jit(solution)/shard_map/ppermute | solution.py:285
  303.9 23.4 %collective-permute-start.66 = (f32[2,6,32,128]{3,2,1,0:T(8,128)S(1)}, f32[2,6,32,128]{3,2,1,0:T(8,128)S(1)}, u32[]{:S(2)}, u32[]{:S(2)}) collective-permute-start(f32[2,6,32,128]{3,2,1,0:T(8,128)S(1)} %get-tuple-element.260), channel_id=1, source_target_pairs={{0,24},{2,26},{4,28},{6,30},{8,16},{10,18},{12,20},{14,22},{16,8},... | collective-permute-start | bytes 589832 | tf_op jit(solution)/shard_map/ppermute | solution.py:285
  (49 other events, 668.9 us)

commit v4 on v3

--- a/solution.py
+++ b/solution.py
@@ -39,9 +39,11 @@
     third = lookup(tables[3:4], index)
     remainder = entries - shift
     t = remainder * inverse(first)
+    triple = 3.0 * third
+    double = 2.0 * third
     for _ in range(NEWTON):
-        u = third * (t * t)
-        t = (2.0 * u * t + remainder) * inverse(first + 3.0 * u)
+        square = t * t
+        t = (double * square * t + remainder) * inverse(first + triple * square)
     return base + t
 
 

time: 341 us -> 342 us (level)
  starting transfers between devices: 102 us -> 108 us
  waiting for transfers between devices: 155 us -> 149 us
    ppermute x56, waiting for transfers between devices: 142 us -> 135 us  [between_chips(): moved[p] = lax.ppermute(x, 'wall', [(i, i ^ 2 * p) for i in range(n)])]
    ppermute x56, starting transfers between devices: 89.8 us -> 96.1 us  [between_chips(): moved[p] = lax.ppermute(x, 'wall', [(i, i ^ 2 * p) for i in range(n)])]
  transfers between devices with their start and end apart: 68 -> 68, of which waited for: 32 -> 32; matrix products, arithmetic and copies ran while one was open for 0% -> 0% of each run, Pallas kernels for 15% -> 16%
where the time goes in v4:
time: 342 us; the launch traced here: 336 us
  waiting for transfers between devices  149 us (44%)
  starting transfers between devices  108 us (32%)
  Pallas kernels  74.2 us (22%)
  local copies, waits for them, and re-layouts  3.79 us (1%)
    ppermute x56, waiting for transfers between devices, between_chips(): moved[p] = lax.ppermute(x, 'wall', [(i, i ^ 2 * p) for i in range(n)])  135 us
    ppermute x56, starting transfers between devices, between_chips(): moved[p] = lax.ppermute(x, 'wall', [(i, i ^ 2 * p) for i in range(n)])  96.1 us
    pallas_call x2, Pallas kernels, middle(): call(functools.partial(middle_kernel, chips), [whole_spec(c), whole_spec(...  24.1 us
    pallas_call x4, Pallas kernels, wall_operator(): call(functools.partial(wall_kernel, chips), [block(w_hi.shape)] * 2 + [bl...  22.2 us
    pallas_call x2, Pallas kernels, first(): call(first_kernel, [whole_spec(c), whole_spec(c), table_spec], [half_spec...  15.9 us
    pallas_call x2, Pallas kernels, last(): call(functools.partial(last_kernel, chips), [half_spec, half_spec, edge_s...  11.4 us
    ppermute x4, waiting for transfers between devices, neighbours(): return lax.ppermute(e, 'span', forward)  7.7 us
  transfers between devices with their start and end apart: 68, of which 32 were waited for; matrix products, arithmetic and copies ran while one was open for 0% of the time, Pallas kernels for 16%

profile of v4, /device:TPU:11, one launch (start us, length us, event | category | flops | bytes accessed | tf_op | source)
XLA Modules:
  0.0 336.3 jit_solution(14166558101886033682)
XLA Ops:
  5.2 7.9 %first.2 = (f32[8,6,32,128]{3,2,1,0:T(8,128)S(1)}, f32[8,6,32,128]{3,2,1,0:T(8,128)S(1)}, f32[6,8,512]{2,1,0:T(8,128)S(1)}) custom-call(s32[2]{0:T(128)S(1)} %pad_add_fusion.me_ref, f32[8,2,12,32,128]{4,3,2,1,0:T(8,128)S(1)} %bitcast.10, s32[8,2,12,32,128]{4,3,2,1,0:T(8,128)S(1)} %bitcast.14, f32[8,128]{1,0:T(8,128)S(1)} %select_maximum_fusion.tab_ref), custom_call_target="tpu_custom_call" | custom-call | flops 1 | bytes 1 | tf_op jit(solution)/shard_map/first/pallas_call | solution.py:232
  15.9 7.9 %first.3 = (f32[8,6,32,128]{3,2,1,0:T(8,128)S(1)}, f32[8,6,32,128]{3,2,1,0:T(8,128)S(1)}, f32[6,8,512]{2,1,0:T(8,128)S(1)}) custom-call(s32[2]{0:T(128)S(1)} %pad_add_fusion.me_ref, f32[8,2,12,32,128]{4,3,2,1,0:T(8,128)S(1)} %bitcast.11, s32[8,2,12,32,128]{4,3,2,1,0:T(8,128)S(1)} %bitcast.15, f32[8,128]{1,0:T(8,128)S(1)} %select_maximum_fusion.tab_ref), custom_call_target="tpu_custom_call" | custom-call | flops 1 | bytes 1 | tf_op jit(solution)/shard_map/first/pallas_call | solution.py:232
  28.2 7.3 %collective-permute-done.5.refs_3_ = f32[2,6,32,128]{3,2,1,0:T(8,128)S(1)} collective-permute-done((f32[2,6,32,128]{3,2,1,0:T(8,128)S(1)}, f32[2,6,32,128]{3,2,1,0:T(8,128)S(1)}, u32[]{:S(2)}, u32[]{:S(2)}) %collective-permute-start.5) | collective-permute-done | bytes 196640 | tf_op jit(solution)/shard_map/ppermute | solution.py:287
  41.4 8.5 %collective-permute-done.10.refs_6_ = f32[2,6,32,128]{3,2,1,0:T(8,128)S(1)} collective-permute-done((f32[2,6,32,128]{3,2,1,0:T(8,128)S(1)}, f32[2,6,32,128]{3,2,1,0:T(8,128)S(1)}, u32[]{:S(2)}, u32[]{:S(2)}) %collective-permute-start.10) | collective-permute-done | bytes 196640 | tf_op jit(solution)/shard_map/ppermute | solution.py:287
  56.9 14.1 %collective-permute-done.11.refs_4_ = f32[2,6,32,128]{3,2,1,0:T(8,128)S(1)} collective-permute-done((f32[2,6,32,128]{3,2,1,0:T(8,128)S(1)}, f32[2,6,32,128]{3,2,1,0:T(8,128)S(1)}, u32[]{:S(2)}, u32[]{:S(2)}) %collective-permute-start.11) | collective-permute-done | bytes 196640 | tf_op jit(solution)/shard_map/ppermute | solution.py:287
  72.4 5.5 %wall.4 = (f32[2,6,32,128]{3,2,1,0:T(8,128)S(1)}, f32[2,6,32,128]{3,2,1,0:T(8,128)S(1)}, f32[2,6,32,128]{3,2,1,0:T(8,128)S(1)}, f32[2,6,32,128]{3,2,1,0:T(8,128)...) custom-call(s32[2]{0:T(128)S(1)} %pad_add_fusion.me_ref, ...), custom_call_target="tpu_custom_call" | custom-call | flops 1 | bytes 1 | tf_op jit(solution)/shard_map/wall/pallas_call | solution.py:256
  87.1 6.4 %collective-permute-done.17.refs_5_ = f32[2,6,32,128]{3,2,1,0:T(8,128)S(1)} collective-permute-done((f32[2,6,32,128]{3,2,1,0:T(8,128)S(1)}, f32[2,6,32,128]{3,2,1,0:T(8,128)S(1)}, u32[]{:S(2)}, u32[]{:S(2)}) %collective-permute-start.17) | collective-permute-done | bytes 196640 | tf_op jit(solution)/shard_map/ppermute | solution.py:287
  105.6 5.5 %wall.5 = (f32[2,6,32,128]{3,2,1,0:T(8,128)S(1)}, f32[2,6,32,128]{3,2,1,0:T(8,128)S(1)}, f32[2,6,32,128]{3,2,1,0:T(8,128)S(1)}, f32[2,6,32,128]{3,2,1,0:T(8,128)...) custom-call(s32[2]{0:T(128)S(1)} %pad_add_fusion.me_ref, ...), custom_call_target="tpu_custom_call" | custom-call | flops 1 | bytes 1 | tf_op jit(solution)/shard_map/wall/pallas_call | solution.py:256
  112.3 8.6 %collective-permute-start.23 = (f32[2,6,32,128]{3,2,1,0:T(8,128)S(1)}, f32[2,6,32,128]{3,2,1,0:T(8,128)S(1)}, u32[]{:S(2)}, u32[]{:S(2)}) collective-permute-start(f32[2,6,32,128]{3,2,1,0:T(8,128)S(1)} %get-tuple-element.178), channel_id=1, source_target_pairs={{0,12},{2,14},{4,8},{6,10},{8,4},{10,6},{12,0},{14,2},{16,28},{18,... | collective-permute-start | bytes 589832 | tf_op jit(solution)/shard_map/ppermute | solution.py:287
  122.3 5.6 %collective-permute-done.23.refs_3_ = f32[2,6,32,128]{3,2,1,0:T(8,128)S(1)} collective-permute-done((f32[2,6,32,128]{3,2,1,0:T(8,128)S(1)}, f32[2,6,32,128]{3,2,1,0:T(8,128)S(1)}, u32[]{:S(2)}, u32[]{:S(2)}) %collective-permute-start.23) | collective-permute-done | bytes 196640 | tf_op jit(solution)/shard_map/ppermute | solution.py:287
  137.0 7.2 %collective-permute-done.30.refs_7_ = f32[2,6,32,128]{3,2,1,0:T(8,128)S(1)} collective-permute-done((f32[2,6,32,128]{3,2,1,0:T(8,128)S(1)}, f32[2,6,32,128]{3,2,1,0:T(8,128)S(1)}, u32[]{:S(2)}, u32[]{:S(2)}) %collective-permute-start.30) | collective-permute-done | bytes 196640 | tf_op jit(solution)/shard_map/ppermute | solution.py:287
  151.4 12.0 %middle.2 = (f32[8,6,32,128]{3,2,1,0:T(8,128)S(1)}, f32[8,6,32,128]{3,2,1,0:T(8,128)S(1)}, f32[2,8,6,32,128]{4,3,2,1,0:T(8,128)S(1)}, f32[6,8,512]{2,1,0:T(8,128)S(1)}) custom-call(s32[2]{0:T(128)S(1)} %pad_add_fusion.me_ref, f32[8,2,12,32,128]{4,3,2,1,0:T(8,128)S(1)} %bitcast.12, s32[8,2,12,32,128]{4,3,2,1,0:T(8,128)S(1)} %bitcast.16, ...), custom_call_target="tpu_custom_call" | custom-call | flops 1 | bytes 1 | tf_op jit(solution)/shard_map/middle/pallas_call | solution.py:238
  172.8 12.2 %middle.3 = (f32[8,6,32,128]{3,2,1,0:T(8,128)S(1)}, f32[8,6,32,128]{3,2,1,0:T(8,128)S(1)}, f32[2,8,6,32,128]{4,3,2,1,0:T(8,128)S(1)}, f32[6,8,512]{2,1,0:T(8,128)S(1)}) custom-call(s32[2]{0:T(128)S(1)} %pad_add_fusion.me_ref, f32[8,2,12,32,128]{4,3,2,1,0:T(8,128)S(1)} %bitcast.13, s32[8,2,12,32,128]{4,3,2,1,0:T(8,128)S(1)} %bitcast.17, ...), custom_call_target="tpu_custom_call" | custom-call | flops 1 | bytes 1 | tf_op jit(solution)/shard_map/middle/pallas_call | solution.py:238
  189.5 10.7 %collective-permute-done.39.refs_3_ = f32[2,6,32,128]{3,2,1,0:T(8,128)S(1)} collective-permute-done((f32[2,6,32,128]{3,2,1,0:T(8,128)S(1)}, f32[2,6,32,128]{3,2,1,0:T(8,128)S(1)}, u32[]{:S(2)}, u32[]{:S(2)}) %collective-permute-start.39) | collective-permute-done | bytes 196640 | tf_op jit(solution)/shard_map/ppermute | solution.py:287
  215.4 7.9 %collective-permute-done.45.refs_4_ = f32[2,6,32,128]{3,2,1,0:T(8,128)S(1)} collective-permute-done((f32[2,6,32,128]{3,2,1,0:T(8,128)S(1)}, f32[2,6,32,128]{3,2,1,0:T(8,128)S(1)}, u32[]{:S(2)}, u32[]{:S(2)}) %collective-permute-start.45) | collective-permute-done | bytes 196640 | tf_op jit(solution)/shard_map/ppermute | solution.py:287
  223.3 9.6 %collective-permute-start.47 = (f32[2,6,32,128]{3,2,1,0:T(8,128)S(1)}, f32[2,6,32,128]{3,2,1,0:T(8,128)S(1)}, u32[]{:S(2)}, u32[]{:S(2)}) collective-permute-start(f32[2,6,32,128]{3,2,1,0:T(8,128)S(1)} %get-tuple-element.221), channel_id=1, source_target_pairs={{0,8},{2,10},{4,12},{6,14},{8,0},{10,2},{12,4},{14,6},{16,24},{18,... | collective-permute-start | bytes 589832 | tf_op jit(solution)/shard_map/ppermute | solution.py:287
  232.9 5.5 %wall.6 = (f32[2,6,32,128]{3,2,1,0:T(8,128)S(1)}, f32[2,6,32,128]{3,2,1,0:T(8,128)S(1)}, f32[2,6,32,128]{3,2,1,0:T(8,128)S(1)}, f32[2,6,32,128]{3,2,1,0:T(8,128)...) custom-call(s32[2]{0:T(128)S(1)} %pad_add_fusion.me_ref, ...), custom_call_target="tpu_custom_call" | custom-call | flops 1 | bytes 1 | tf_op jit(solution)/shard_map/wall/pallas_call | solution.py:256
  246.7 6.4 %collective-permute-done.51.refs_5_ = f32[2,6,32,128]{3,2,1,0:T(8,128)S(1)} collective-permute-done((f32[2,6,32,128]{3,2,1,0:T(8,128)S(1)}, f32[2,6,32,128]{3,2,1,0:T(8,128)S(1)}, u32[]{:S(2)}, u32[]{:S(2)}) %collective-permute-start.51) | collective-permute-done | bytes 196640 | tf_op jit(solution)/shard_map/ppermute | solution.py:287
  265.1 5.5 %wall.7 = (f32[2,6,32,128]{3,2,1,0:T(8,128)S(1)}, f32[2,6,32,128]{3,2,1,0:T(8,128)S(1)}, f32[2,6,32,128]{3,2,1,0:T(8,128)S(1)}, f32[2,6,32,128]{3,2,1,0:T(8,128)...) custom-call(s32[2]{0:T(128)S(1)} %pad_add_fusion.me_ref, ...), custom_call_target="tpu_custom_call" | custom-call | flops 1 | bytes 1 | tf_op jit(solution)/shard_map/wall/pallas_call | solution.py:256
  271.6 5.9 %collective-permute-done.56.refs_2_ = f32[2,6,32,128]{3,2,1,0:T(8,128)S(1)} collective-permute-done((f32[2,6,32,128]{3,2,1,0:T(8,128)S(1)}, f32[2,6,32,128]{3,2,1,0:T(8,128)S(1)}, u32[]{:S(2)}, u32[]{:S(2)}) %collective-permute-start.56) | collective-permute-done | bytes 196640 | tf_op jit(solution)/shard_map/ppermute | solution.py:287
  298.4 5.8 %collective-permute-start.65 = (f32[2,6,32,128]{3,2,1,0:T(8,128)S(1)}, f32[2,6,32,128]{3,2,1,0:T(8,128)S(1)}, u32[]{:S(2)}, u32[]{:S(2)}) collective-permute-start(f32[2,6,32,128]{3,2,1,0:T(8,128)S(1)} %get-tuple-element.258), channel_id=1, source_target_pairs={{0,20},{2,22},{4,16},{6,18},{8,28},{10,30},{12,24},{14,26},{16,4},... | collective-permute-start | bytes 589832 | tf_op jit(solution)/shard_map/ppermute | solution.py:287
  311.0 5.7 %last.2 = (f32[8,2,12,32,128]{4,3,2,1,0:T(8,128)}, f32[8,2,12,32,128]{4,3,2,1,0:T(8,128)}) custom-call(s32[2]{0:T(128)S(1)} %pad_add_fusion.me_ref, f32[8,6,32,128]{3,2,1,0:T(8,128)S(1)} %get-tuple-element.183.same_ref, f32[8,6,32,128]{3,2,1,0:T(8,128)S(1)} %get-tuple-element.201.other_ref, f32[6,8,512]{2,1,0:T(8,128)S(1)} %collective-permute-done.42.halo_ref, ...), custom_call_target="tpu_custom_call" | custom-call | flops 1 | bytes 1 | tf_op jit(solution)/shard_map/last/pallas_call | solution.py:245
  321.9 5.8 %collective-permute-done.66.refs_6_ = f32[2,6,32,128]{3,2,1,0:T(8,128)S(1)} collective-permute-done((f32[2,6,32,128]{3,2,1,0:T(8,128)S(1)}, f32[2,6,32,128]{3,2,1,0:T(8,128)S(1)}, u32[]{:S(2)}, u32[]{:S(2)}) %collective-permute-start.66) | collective-permute-done | bytes 196640 | tf_op jit(solution)/shard_map/ppermute | solution.py:287
  330.6 5.7 %last.3 = (f32[8,2,12,32,128]{4,3,2,1,0:T(8,128)}, f32[8,2,12,32,128]{4,3,2,1,0:T(8,128)}) custom-call(s32[2]{0:T(128)S(1)} %pad_add_fusion.me_ref, f32[8,6,32,128]{3,2,1,0:T(8,128)S(1)} %get-tuple-element.195.same_ref, f32[8,6,32,128]{3,2,1,0:T(8,128)S(1)} %get-tuple-element.196.other_ref, ...), custom_call_target="tpu_custom_call", output_to_operand_aliasing={{0}: (14, {}), {1}: (15, {})} | custom-call | flops 1 | bytes 1 | tf_op jit(solution)/shard_map/last/pallas_call | solution.py:245
  (143 shorter events, 152.2 us)
Async XLA Ops:
  23.9 26.1 %collective-permute-start.2 = (f32[8,6,32,128]{3,2,1,0:T(8,128)S(1)}, f32[8,6,32,128]{3,2,1,0:T(8,128)S(1)}, u32[]{:S(2)}, u32[]{:S(2)}) collective-permute-start(f32[8,6,32,128]{3,2,1,0:T(8,128)S(1)} %get-tuple-element.138.other_ref), channel_id=1, source_target_pairs={{0,2},{2,0},{4,6},{6,4},{8,10},{10,8},{12,14},{14,12},{16,18},{18,... | collective-permute-start | bytes 2359304 | tf_op jit(solution)/shard_map/ppermute | solution.py:293
  28.0 21.9 %collective-permute-start.10 = (f32[2,6,32,128]{3,2,1,0:T(8,128)S(1)}, f32[2,6,32,128]{3,2,1,0:T(8,128)S(1)}, u32[]{:S(2)}, u32[]{:S(2)}) collective-permute-start(f32[2,6,32,128]{3,2,1,0:T(8,128)S(1)} %get-tuple-element.151), channel_id=1, source_target_pairs={{0,28},{2,30},{4,24},{6,26},{8,20},{10,22},{12,16},{14,18},{16,12}... | collective-permute-start | bytes 589832 | tf_op jit(solution)/shard_map/ppermute | solution.py:287
  35.9 36.4 %collective-permute-start.9 = (f32[2,6,32,128]{3,2,1,0:T(8,128)S(1)}, f32[2,6,32,128]{3,2,1,0:T(8,128)S(1)}, u32[]{:S(2)}, u32[]{:S(2)}) collective-permute-start(f32[2,6,32,128]{3,2,1,0:T(8,128)S(1)} %get-tuple-element.149), channel_id=1, source_target_pairs={{0,12},{2,14},{4,8},{6,10},{8,4},{10,6},{12,0},{14,2},{16,28},{18,... | collective-permute-start | bytes 589832 | tf_op jit(solution)/shard_map/ppermute | solution.py:287
  49.9 21.1 %collective-permute-start.11 = (f32[2,6,32,128]{3,2,1,0:T(8,128)S(1)}, f32[2,6,32,128]{3,2,1,0:T(8,128)S(1)}, u32[]{:S(2)}, u32[]{:S(2)}) collective-permute-start(f32[2,6,32,128]{3,2,1,0:T(8,128)S(1)} %get-tuple-element.152), channel_id=1, source_target_pairs={{0,20},{2,22},{4,16},{6,18},{8,28},{10,30},{12,24},{14,26},{16,4},... | collective-permute-start | bytes 589832 | tf_op jit(solution)/shard_map/ppermute | solution.py:287
  54.2 25.8 %collective-permute-start.15 = (f32[2,6,32,128]{3,2,1,0:T(8,128)S(1)}, f32[2,6,32,128]{3,2,1,0:T(8,128)S(1)}, u32[]{:S(2)}, u32[]{:S(2)}) collective-permute-start(f32[2,6,32,128]{3,2,1,0:T(8,128)S(1)} %get-tuple-element.161), channel_id=1, source_target_pairs={{0,28},{2,30},{4,24},{6,26},{8,20},{10,22},{12,16},{14,18},{16,12}... | collective-permute-start | bytes 589832 | tf_op jit(solution)/shard_map/ppermute | solution.py:287
  56.3 24.4 %collective-permute-start.4 = (f32[2,6,32,128]{3,2,1,0:T(8,128)S(1)}, f32[2,6,32,128]{3,2,1,0:T(8,128)S(1)}, u32[]{:S(2)}, u32[]{:S(2)}) collective-permute-start(f32[2,6,32,128]{3,2,1,0:T(8,128)S(1)} %get-tuple-element.143), channel_id=1, source_target_pairs={{0,16},{2,18},{4,20},{6,22},{8,24},{10,26},{12,28},{14,30},{16,0},... | collective-permute-start | bytes 589832 | tf_op jit(solution)/shard_map/ppermute | solution.py:287
  80.7 23.3 %collective-permute-start.12 = (f32[2,6,32,128]{3,2,1,0:T(8,128)S(1)}, f32[2,6,32,128]{3,2,1,0:T(8,128)S(1)}, u32[]{:S(2)}, u32[]{:S(2)}) collective-permute-start(f32[2,6,32,128]{3,2,1,0:T(8,128)S(1)} %get-tuple-element.154), channel_id=1, source_target_pairs={{0,4},{2,6},{4,0},{6,2},{8,12},{10,14},{12,8},{14,10},{16,20},{18,... | collective-permute-start | bytes 589832 | tf_op jit(solution)/shard_map/ppermute | solution.py:287
  85.1 20.0 %collective-permute-start.14 = (f32[2,6,32,128]{3,2,1,0:T(8,128)S(1)}, f32[2,6,32,128]{3,2,1,0:T(8,128)S(1)}, u32[]{:S(2)}, u32[]{:S(2)}) collective-permute-start(f32[2,6,32,128]{3,2,1,0:T(8,128)S(1)} %get-tuple-element.158), channel_id=1, source_target_pairs={{0,12},{2,14},{4,8},{6,10},{8,4},{10,6},{12,0},{14,2},{16,28},{18,... | collective-permute-start | bytes 589832 | tf_op jit(solution)/shard_map/ppermute | solution.py:287
  131.4 20.0 %collective-permute-start.26 = (f32[8,6,32,128]{3,2,1,0:T(8,128)S(1)}, f32[8,6,32,128]{3,2,1,0:T(8,128)S(1)}, u32[]{:S(2)}, u32[]{:S(2)}) collective-permute-start(f32[8,6,32,128]{3,2,1,0:T(8,128)S(1)} %gather.4), channel_id=1, source_target_pairs={{0,2},{2,0},{4,6},{6,4},{8,10},{10,8},{12,14},{14,12},{16,18},{18,... | collective-permute-start | bytes 2359304 | tf_op jit(solution)/shard_map/ppermute | solution.py:293
  137.0 26.4 %collective-permute-start.19 = (f32[2,6,32,128]{3,2,1,0:T(8,128)S(1)}, f32[2,6,32,128]{3,2,1,0:T(8,128)S(1)}, u32[]{:S(2)}, u32[]{:S(2)}) collective-permute-start(f32[2,6,32,128]{3,2,1,0:T(8,128)S(1)} %get-tuple-element.170), channel_id=1, source_target_pairs={{0,16},{2,18},{4,20},{6,22},{8,24},{10,26},{12,28},{14,30},{16,0},... | collective-permute-start | bytes 589832 | tf_op jit(solution)/shard_map/ppermute | solution.py:287
  144.2 19.9 %collective-permute-start.31 = (f32[2,6,32,128]{3,2,1,0:T(8,128)S(1)}, f32[2,6,32,128]{3,2,1,0:T(8,128)S(1)}, u32[]{:S(2)}, u32[]{:S(2)}) collective-permute-start(f32[2,6,32,128]{3,2,1,0:T(8,128)S(1)} %get-tuple-element.192), channel_id=1, source_target_pairs={{0,20},{2,22},{4,16},{6,18},{8,28},{10,30},{12,24},{14,26},{16,4},... | collective-permute-start | bytes 589832 | tf_op jit(solution)/shard_map/ppermute | solution.py:287
  145.0 23.8 %collective-permute-start.32 = (f32[2,6,32,128]{3,2,1,0:T(8,128)S(1)}, f32[2,6,32,128]{3,2,1,0:T(8,128)S(1)}, u32[]{:S(2)}, u32[]{:S(2)}) collective-permute-start(f32[2,6,32,128]{3,2,1,0:T(8,128)S(1)} %get-tuple-element.194), channel_id=1, source_target_pairs={{0,24},{2,26},{4,28},{6,30},{8,16},{10,18},{12,20},{14,22},{16,8},... | collective-permute-start | bytes 589832 | tf_op jit(solution)/shard_map/ppermute | solution.py:287
  148.6 20.2 %collective-permute-start.29 = (f32[2,6,32,128]{3,2,1,0:T(8,128)S(1)}, f32[2,6,32,128]{3,2,1,0:T(8,128)S(1)}, u32[]{:S(2)}, u32[]{:S(2)}) collective-permute-start(f32[2,6,32,128]{3,2,1,0:T(8,128)S(1)} %get-tuple-element.188), channel_id=1, source_target_pairs={{0,12},{2,14},{4,8},{6,10},{8,4},{10,6},{12,0},{14,2},{16,28},{18,... | collective-permute-start | bytes 589832 | tf_op jit(solution)/shard_map/ppermute | solution.py:287
  185.0 28.2 %collective-permute-start.35 = (f32[8,6,32,128]{3,2,1,0:T(8,128)S(1)}, f32[8,6,32,128]{3,2,1,0:T(8,128)S(1)}, u32[]{:S(2)}, u32[]{:S(2)}) collective-permute-start(f32[8,6,32,128]{3,2,1,0:T(8,128)S(1)} %get-tuple-element.196.other_ref), channel_id=1, source_target_pairs={{0,2},{2,0},{4,6},{6,4},{8,10},{10,8},{12,14},{14,12},{16,18},{18,... | collective-permute-start | bytes 2359304 | tf_op jit(solution)/shard_map/ppermute | solution.py:293
  189.5 20.7 %collective-permute-start.41 = (f32[2,6,32,128]{3,2,1,0:T(8,128)S(1)}, f32[2,6,32,128]{3,2,1,0:T(8,128)S(1)}, u32[]{:S(2)}, u32[]{:S(2)}) collective-permute-start(f32[2,6,32,128]{3,2,1,0:T(8,128)S(1)} %get-tuple-element.210), channel_id=1, source_target_pairs={{0,8},{2,10},{4,12},{6,14},{8,0},{10,2},{12,4},{14,6},{16,24},{18,... | collective-permute-start | bytes 589832 | tf_op jit(solution)/shard_map/ppermute | solution.py:287
  210.2 22.7 %collective-permute-start.43 = (f32[2,6,32,128]{3,2,1,0:T(8,128)S(1)}, f32[2,6,32,128]{3,2,1,0:T(8,128)S(1)}, u32[]{:S(2)}, u32[]{:S(2)}) collective-permute-start(f32[2,6,32,128]{3,2,1,0:T(8,128)S(1)} %get-tuple-element.213), channel_id=1, source_target_pairs={{0,12},{2,14},{4,8},{6,10},{8,4},{10,6},{12,0},{14,2},{16,28},{18,... | collective-permute-start | bytes 589832 | tf_op jit(solution)/shard_map/ppermute | solution.py:287
  213.3 26.1 %collective-permute-start.49 = (f32[2,6,32,128]{3,2,1,0:T(8,128)S(1)}, f32[2,6,32,128]{3,2,1,0:T(8,128)S(1)}, u32[]{:S(2)}, u32[]{:S(2)}) collective-permute-start(f32[2,6,32,128]{3,2,1,0:T(8,128)S(1)} %get-tuple-element.226), channel_id=1, source_target_pairs={{0,28},{2,30},{4,24},{6,26},{8,20},{10,22},{12,16},{14,18},{16,12}... | collective-permute-start | bytes 589832 | tf_op jit(solution)/shard_map/ppermute | solution.py:287
  214.5 26.7 %collective-permute-start.38 = (f32[2,6,32,128]{3,2,1,0:T(8,128)S(1)}, f32[2,6,32,128]{3,2,1,0:T(8,128)S(1)}, u32[]{:S(2)}, u32[]{:S(2)}) collective-permute-start(f32[2,6,32,128]{3,2,1,0:T(8,128)S(1)} %get-tuple-element.204), channel_id=1, source_target_pairs={{0,16},{2,18},{4,20},{6,22},{8,24},{10,26},{12,28},{14,30},{16,0},... | collective-permute-start | bytes 589832 | tf_op jit(solution)/shard_map/ppermute | solution.py:287
  223.3 22.2 %collective-permute-start.47 = (f32[2,6,32,128]{3,2,1,0:T(8,128)S(1)}, f32[2,6,32,128]{3,2,1,0:T(8,128)S(1)}, u32[]{:S(2)}, u32[]{:S(2)}) collective-permute-start(f32[2,6,32,128]{3,2,1,0:T(8,128)S(1)} %get-tuple-element.221), channel_id=1, source_target_pairs={{0,8},{2,10},{4,12},{6,14},{8,0},{10,2},{12,4},{14,6},{16,24},{18,... | collective-permute-start | bytes 589832 | tf_op jit(solution)/shard_map/ppermute | solution.py:287
  241.2 22.1 %collective-permute-start.46 = (f32[2,6,32,128]{3,2,1,0:T(8,128)S(1)}, f32[2,6,32,128]{3,2,1,0:T(8,128)S(1)}, u32[]{:S(2)}, u32[]{:S(2)}) collective-permute-start(f32[2,6,32,128]{3,2,1,0:T(8,128)S(1)} %get-tuple-element.219), channel_id=1, source_target_pairs={{0,4},{2,6},{4,0},{6,2},{8,12},{10,14},{12,8},{14,10},{16,20},{18,... | collective-permute-start | bytes 589832 | tf_op jit(solution)/shard_map/ppermute | solution.py:287
  289.7 21.2 %collective-permute-start.60 = (f32[8,6,32,128]{3,2,1,0:T(8,128)S(1)}, f32[8,6,32,128]{3,2,1,0:T(8,128)S(1)}, u32[]{:S(2)}, u32[]{:S(2)}) collective-permute-start(f32[8,6,32,128]{3,2,1,0:T(8,128)S(1)} %gather.6), channel_id=1, source_target_pairs={{0,2},{2,0},{4,6},{6,4},{8,10},{10,8},{12,14},{14,12},{16,18},{18,... | collective-permute-start | bytes 2359304 | tf_op jit(solution)/shard_map/ppermute | solution.py:293
  296.2 20.4 %collective-permute-start.53 = (f32[2,6,32,128]{3,2,1,0:T(8,128)S(1)}, f32[2,6,32,128]{3,2,1,0:T(8,128)S(1)}, u32[]{:S(2)}, u32[]{:S(2)}) collective-permute-start(f32[2,6,32,128]{3,2,1,0:T(8,128)S(1)} %get-tuple-element.235), channel_id=1, source_target_pairs={{0,16},{2,18},{4,20},{6,22},{8,24},{10,26},{12,28},{14,30},{16,0},... | collective-permute-start | bytes 589832 | tf_op jit(solution)/shard_map/ppermute | solution.py:287
  298.4 23.5 %collective-permute-start.65 = (f32[2,6,32,128]{3,2,1,0:T(8,128)S(1)}, f32[2,6,32,128]{3,2,1,0:T(8,128)S(1)}, u32[]{:S(2)}, u32[]{:S(2)}) collective-permute-start(f32[2,6,32,128]{3,2,1,0:T(8,128)S(1)} %get-tuple-element.258), channel_id=1, source_target_pairs={{0,20},{2,22},{4,16},{6,18},{8,28},{10,30},{12,24},{14,26},{16,4},... | collective-permute-start | bytes 589832 | tf_op jit(solution)/shard_map/ppermute | solution.py:287
  304.3 23.5 %collective-permute-start.66 = (f32[2,6,32,128]{3,2,1,0:T(8,128)S(1)}, f32[2,6,32,128]{3,2,1,0:T(8,128)S(1)}, u32[]{:S(2)}, u32[]{:S(2)}) collective-permute-start(f32[2,6,32,128]{3,2,1,0:T(8,128)S(1)} %get-tuple-element.260), channel_id=1, source_target_pairs={{0,24},{2,26},{4,28},{6,30},{8,16},{10,18},{12,20},{14,22},{16,8},... | collective-permute-start | bytes 589832 | tf_op jit(solution)/shard_map/ppermute | solution.py:287
  (49 other events, 666.3 us)
